TPU v7x, 32 devices: a whole 2x2x4 slice. The times are simulated.
32 devices in a mesh: sa: 4 (over z), sb: 8 (over y, x, core).
Axes of the slice: x: 2, y: 2, z: 4, core: 2. Of those that a mesh axis runs over, the one named last changes fastest.
Arguments:
- queries: float32 [8192, 128], P(('sa', 'sb')), may hold values from -6 to 6
- keys: float32 [8192, 128], P(('sa', 'sb')), may hold values from -6 to 6
- values: float32 [8192, 128], P(('sa', 'sb')), may hold values from -6 to 6
- cotangent: float32 [8192, 128], P(('sa', 'sb')), may hold values from -6 to 6
- filt: float32 [8192, 128], P(('sa', 'sb')), may hold values from -6 to 6
- skip: float32 [128], replicated, may hold values from -4 to 4
Outputs:
- grad_queries: float32 [8192, 128], P(('sa', 'sb'))
- grad_keys: float32 [8192, 128], P(('sa', 'sb'))
- grad_values: float32 [8192, 128], P(('sa', 'sb'))
- grad_filter: float32 [8192, 128], P(('sa', 'sb'))
All inputs are finite; a program needn't handle non-finite values.
Results may differ from a plain program's by a relative error of at most 0.000098.
Values sent between devices are 32-bit elements; how exact they have to be, the bound alone decides.
No kernel may reach another device: no remote copies, remote signals or barrier semaphores. Data moves between devices by JAX's collectives and lax.ppermute only.
A program may use at most 64 MiB of HBM per device.

v0:
```python
import math

import jax
import jax.numpy as jnp
from jax import lax
from jax.sharding import PartitionSpec as P

highest = lax.Precision.HIGHEST


def phase_pair(count, period, direction):
    turned = count % period
    angle = 2.0 * math.pi / period * turned.astype(jnp.float32)
    return (jnp.cos(angle), direction * jnp.sin(angle))


def table(extent, direction):
    numbers = jnp.arange(extent, dtype=jnp.int32)
    return phase_pair(numbers[:, None] * numbers[None, :], extent, direction)


def along(matrices, real_part, imag_part, axis):
    cosine, sine_part = matrices

    def apply(matrix, operand):
        product = jnp.tensordot(matrix, operand, axes=((1,), (axis,)), precision=highest)
        return jnp.moveaxis(product, 0, axis)

    return (
        apply(cosine, real_part) - apply(sine_part, imag_part),
        apply(sine_part, real_part) + apply(cosine, imag_part),
    )


def times(real_part, imag_part, turn_real, turn_imag):
    return (
        real_part * turn_real - imag_part * turn_imag,
        real_part * turn_imag + imag_part * turn_real,
    )


def split_factor(extent):
    first = 1
    for attempt in range(32):
        if 4 * first * first <= extent and extent % (2 * first) == 0:
            first = 2 * first
    return first


def local_dft(real_part, imag_part, direction, axis):
    old_shape = real_part.shape
    extent = old_shape[axis]
    first = split_factor(extent)
    second = extent // first
    new_shape = old_shape[:axis] + (first, second) + old_shape[axis + 1 :]
    real_part = real_part.reshape(new_shape)
    imag_part = imag_part.reshape(new_shape)
    real_part, imag_part = along(table(first, direction), real_part, imag_part, axis)
    low_index = jnp.arange(first, dtype=jnp.int32)
    high_index = jnp.arange(second, dtype=jnp.int32)
    turn_real, turn_imag = phase_pair(low_index[:, None] * high_index[None, :], extent, direction)
    trailing = (1,) * (len(new_shape) - axis - 2)
    turn_real = turn_real.reshape((first, second) + trailing)
    turn_imag = turn_imag.reshape((first, second) + trailing)
    real_part, imag_part = times(real_part, imag_part, turn_real, turn_imag)
    real_part, imag_part = along(table(second, direction), real_part, imag_part, axis + 1)
    real_part = jnp.swapaxes(real_part, axis, axis + 1).reshape(old_shape)
    imag_part = jnp.swapaxes(imag_part, axis, axis + 1).reshape(old_shape)
    return (real_part, imag_part)


def parities(signal, position, length):
    cosine, sine_part = phase_pair(position, 2 * length, -1.0)
    zeros_part = jnp.zeros_like(signal)
    return (jnp.stack([signal, signal * cosine]), jnp.stack([zeros_part, signal * sine_part]))


def combine(real_part, imag_part, position, length, factor):
    cosine, sine_part = phase_pair(position, 2 * length, 1.0)
    return (real_part[0] + cosine * real_part[1] - sine_part * imag_part[1]) * factor


def spectra_products(gated_spectrum, filter_spectrum, upstream_spectrum):
    gated_real, gated_imag = gated_spectrum
    filter_real, filter_imag = filter_spectrum
    upstream_real, upstream_imag = upstream_spectrum
    forward_product = (
        filter_real * gated_real - filter_imag * gated_imag,
        filter_real * gated_imag + filter_imag * gated_real,
    )
    back_product = (
        filter_real * upstream_real + filter_imag * upstream_imag,
        filter_real * upstream_imag - filter_imag * upstream_real,
    )
    filter_product = (
        gated_real * upstream_real + gated_imag * upstream_imag,
        gated_real * upstream_imag - gated_imag * upstream_real,
    )
    return (forward_product, back_product, filter_product)


def local(queries, keys, values, cotangent, filt, skip):
    segment, channels = queries.shape
    devices = lax.axis_size(("sa", "sb"))
    length = segment * devices
    factor = 1.0 / (math.sqrt(length) * 2.0 * length)
    gated = keys * values
    upstream = cotangent * queries
    signals = (gated, filt, upstream)
    device = lax.axis_index(("sa", "sb"))
    piece_size = segment // devices
    offsets = jnp.arange(piece_size, dtype=jnp.int32)
    sources = jnp.arange(devices, dtype=jnp.int32)
    position = (sources[:, None] * segment + device * piece_size + offsets[None, :])[:, :, None]
    spread = []
    blocks = tuple((signal.reshape(devices, piece_size, channels) for signal in signals))
    arrived = lax.all_to_all(blocks, ("sa", "sb"), split_axis=0, concat_axis=0, tiled=True)
    for signal in arrived:
        real_part, imag_part = parities(signal, position, length)
        spread.append(along(table(devices, -1.0), real_part, imag_part, 1))
    within = device * piece_size + offsets
    turn_real, turn_imag = phase_pair(sources[:, None] * within[None, :], length, -1.0)
    turn_real = turn_real[:, :, None]
    turn_imag = turn_imag[:, :, None]
    twisted = []
    for real_part, imag_part in spread:
        real_part, imag_part = times(real_part, imag_part, turn_real, turn_imag)
        twisted.append(real_part)
        twisted.append(imag_part)
    returned = (
        lax.all_to_all(twisted[0], ("sa", "sb"), split_axis=1, concat_axis=1, tiled=True),
        lax.all_to_all(twisted[1], ("sa", "sb"), split_axis=1, concat_axis=1, tiled=True),
        lax.all_to_all(twisted[2], ("sa", "sb"), split_axis=1, concat_axis=1, tiled=True),
        lax.all_to_all(twisted[3], ("sa", "sb"), split_axis=1, concat_axis=1, tiled=True),
        lax.all_to_all(twisted[4], ("sa", "sb"), split_axis=1, concat_axis=1, tiled=True),
        lax.all_to_all(twisted[5], ("sa", "sb"), split_axis=1, concat_axis=1, tiled=True),
    )
    spectra = []
    for number in range(3):
        real_part = returned[2 * number].reshape(2, segment, channels)
        imag_part = returned[2 * number + 1].reshape(2, segment, channels)
        spectra.append(local_dft(real_part, imag_part, -1.0, 1))
    products = spectra_products(spectra[0], spectra[1], spectra[2])
    steps_back = jnp.arange(segment, dtype=jnp.int32)
    back_real, back_imag = phase_pair(steps_back * device, length, 1.0)
    back_real = back_real[:, None]
    back_imag = back_imag[:, None]
    pending = []
    for real_part, imag_part in products:
        real_part, imag_part = local_dft(real_part, imag_part, 1.0, 1)
        real_part, imag_part = times(real_part, imag_part, back_real, back_imag)
        pending.append(real_part.reshape(2, devices, piece_size, channels))
        pending.append(imag_part.reshape(2, devices, piece_size, channels))
    gathered = (
        lax.all_to_all(pending[0], ("sa", "sb"), split_axis=1, concat_axis=1, tiled=True),
        lax.all_to_all(pending[1], ("sa", "sb"), split_axis=1, concat_axis=1, tiled=True),
        lax.all_to_all(pending[2], ("sa", "sb"), split_axis=1, concat_axis=1, tiled=True),
        lax.all_to_all(pending[3], ("sa", "sb"), split_axis=1, concat_axis=1, tiled=True),
        lax.all_to_all(pending[4], ("sa", "sb"), split_axis=1, concat_axis=1, tiled=True),
        lax.all_to_all(pending[5], ("sa", "sb"), split_axis=1, concat_axis=1, tiled=True),
    )
    outputs = []
    for number in range(3):
        real_part, imag_part = along(
            table(devices, 1.0), gathered[2 * number], gathered[2 * number + 1], 1
        )
        outputs.append(combine(real_part, imag_part, position, length, factor))
    finals = (
        lax.all_to_all(outputs[0], ("sa", "sb"), split_axis=0, concat_axis=0, tiled=True),
        lax.all_to_all(outputs[1], ("sa", "sb"), split_axis=0, concat_axis=0, tiled=True),
        lax.all_to_all(outputs[2], ("sa", "sb"), split_axis=0, concat_axis=0, tiled=True),
    )
    forward_conv = finals[0].reshape(segment, channels)
    back_conv = finals[1].reshape(segment, channels)
    filter_conv = finals[2].reshape(segment, channels)
    response = forward_conv + skip * gated
    back_signal = back_conv + skip * upstream
    return (cotangent * response, back_signal * values, back_signal * keys, filter_conv)


def solution(mesh):
    in_specs = (
        P(("sa", "sb"), None),
        P(("sa", "sb"), None),
        P(("sa", "sb"), None),
        P(("sa", "sb"), None),
        P(("sa", "sb"), None),
        P(),
    )
    out_specs = (
        P(("sa", "sb"), None),
        P(("sa", "sb"), None),
        P(("sa", "sb"), None),
        P(("sa", "sb"), None),
    )
    return jax.shard_map(local, mesh=mesh, in_specs=in_specs, out_specs=out_specs, check_vma=False)
```

profile of v0, /device:TPU:1, one launch (start us, length us, event | category | flops | bytes accessed | tf_op | source)
XLA Modules:
  0.0 256.7 jit_solution(17473061717050576688)
XLA Ops:
  0.7 7.1 %all-to-all-start = ((f32[32,8,128]{2,1,0:T(8,128)}), f32[32,8,128]{2,1,0:T(8,128)S(1)}, u32[]{:S(2)}, u32[]{:S(2)}) async-start(f32[32,8,128]{2,1,0:T(8,128)} %bitcast.384), calls=%async_computation | async-start | bytes 262144 | tf_op jit(solution)/shard_map/all_to_all | solution.py:117
  8.5 7.5 %all-to-all-done = f32[32,8,128]{2,1,0:T(8,128)S(1)} async-done(((f32[32,8,128]{2,1,0:T(8,128)}), f32[32,8,128]{2,1,0:T(8,128)S(1)}, u32[]{:S(2)}, u32[]{:S(2)}) %all-to-all-start) | async-done | bytes 131104 | tf_op jit(solution)/shard_map/all_to_all | solution.py:117
  19.2 7.5 %all-to-all-done.9 = f32[32,8,128]{2,1,0:T(8,128)S(1)} async-done(((f32[32,8,128]{2,1,0:T(8,128)}), f32[32,8,128]{2,1,0:T(8,128)S(1)}, u32[]{:S(2)}, u32[]{:S(2)}) %all-to-all-start.9) | async-done | bytes 131104 | tf_op jit(solution)/shard_map/all_to_all | solution.py:117
  29.3 8.3 %all-to-all-done.3 = f32[32,8,128]{2,1,0:T(8,128)S(1)} async-done(((f32[32,8,128]{2,1,0:T(8,128)}), f32[32,8,128]{2,1,0:T(8,128)S(1)}, u32[]{:S(2)}, u32[]{:S(2)}) %all-to-all-start.3) | async-done | bytes 131104 | tf_op jit(solution)/shard_map/all_to_all | solution.py:117
  47.1 9.5 %all-to-all-done.10 = f32[2,32,8,128]{3,2,0,1:T(8,128)S(1)} async-done(((f32[2,32,8,128]{3,2,0,1:T(8,128)}), f32[2,32,8,128]{3,2,0,1:T(8,128)S(1)}, u32[]{:S(2)}, u32[]{:S(2)}) %all-to-all-start.10) | async-done | bytes 262176 | tf_op jit(solution)/shard_map/all_to_all | solution.py:135
  60.4 9.5 %all-to-all-done.1 = f32[2,32,8,128]{3,2,0,1:T(8,128)S(1)} async-done(((f32[2,32,8,128]{3,2,0,1:T(8,128)}), f32[2,32,8,128]{3,2,0,1:T(8,128)S(1)}, u32[]{:S(2)}, u32[]{:S(2)}) %all-to-all-start.1) | async-done | bytes 262176 | tf_op jit(solution)/shard_map/all_to_all | solution.py:133
  76.3 6.8 %all-to-all-done.4 = f32[2,32,8,128]{3,2,0,1:T(8,128)S(1)} async-done(((f32[2,32,8,128]{3,2,0,1:T(8,128)}), f32[2,32,8,128]{3,2,0,1:T(8,128)S(1)}, u32[]{:S(2)}, u32[]{:S(2)}) %all-to-all-start.4) | async-done | bytes 262176 | tf_op jit(solution)/shard_map/all_to_all | solution.py:131
  87.2 9.1 %all-to-all-done.11 = f32[2,32,8,128]{3,2,0,1:T(8,128)S(1)} async-done(((f32[2,32,8,128]{3,2,0,1:T(8,128)}), f32[2,32,8,128]{3,2,0,1:T(8,128)S(1)}, u32[]{:S(2)}, u32[]{:S(2)}) %all-to-all-start.11) | async-done | bytes 262176 | tf_op jit(solution)/shard_map/all_to_all | solution.py:136
  100.3 9.1 %all-to-all-done.5 = f32[2,32,8,128]{3,2,0,1:T(8,128)S(1)} async-done(((f32[2,32,8,128]{3,2,0,1:T(8,128)}), f32[2,32,8,128]{3,2,0,1:T(8,128)S(1)}, u32[]{:S(2)}, u32[]{:S(2)}) %all-to-all-start.5) | async-done | bytes 262176 | tf_op jit(solution)/shard_map/all_to_all | solution.py:132
  109.4 3.0 %all-to-all-start.2 = ((f32[2,32,8,128]{3,2,0,1:T(8,128)}), f32[2,32,8,128]{3,2,0,1:T(8,128)S(1)}, u32[]{:S(2)}, u32[]{:S(2)}) async-start(f32[2,32,8,128]{3,2,0,1:T(8,128)} %copy.112), calls=%async_computation.2 | async-start | bytes 524288 | tf_op jit(solution)/shard_map/all_to_all | solution.py:134
  113.7 8.9 %all-to-all-done.2 = f32[2,32,8,128]{3,2,0,1:T(8,128)S(1)} async-done(((f32[2,32,8,128]{3,2,0,1:T(8,128)}), f32[2,32,8,128]{3,2,0,1:T(8,128)S(1)}, u32[]{:S(2)}, u32[]{:S(2)}) %all-to-all-start.2) | async-done | bytes 262176 | tf_op jit(solution)/shard_map/all_to_all | solution.py:134
  140.9 2.8 %all-to-all-start.16 = ((f32[2,32,8,128]{3,2,0,1:T(8,128)}), f32[2,32,8,128]{3,2,0,1:T(8,128)S(1)}, u32[]{:S(2)}, u32[]{:S(2)}) async-start(f32[2,32,8,128]{3,2,0,1:T(8,128)} %copy.190), calls=%async_computation.16 | async-start | bytes 524288 | tf_op jit(solution)/shard_map/all_to_all | solution.py:160
  144.4 9.7 %all-to-all-done.16 = f32[2,32,8,128]{3,2,0,1:T(8,128)S(1)} async-done(((f32[2,32,8,128]{3,2,0,1:T(8,128)}), f32[2,32,8,128]{3,2,0,1:T(8,128)S(1)}, u32[]{:S(2)}, u32[]{:S(2)}) %all-to-all-start.16) | async-done | bytes 262176 | tf_op jit(solution)/shard_map/all_to_all | solution.py:160
  154.1 2.8 %all-to-all-start.15 = ((f32[2,32,8,128]{3,2,0,1:T(8,128)}), f32[2,32,8,128]{3,2,0,1:T(8,128)S(1)}, u32[]{:S(2)}, u32[]{:S(2)}) async-start(f32[2,32,8,128]{3,2,0,1:T(8,128)} %copy.188), calls=%async_computation.15 | async-start | bytes 524288 | tf_op jit(solution)/shard_map/all_to_all | solution.py:159
  157.6 9.7 %all-to-all-done.15 = f32[2,32,8,128]{3,2,0,1:T(8,128)S(1)} async-done(((f32[2,32,8,128]{3,2,0,1:T(8,128)}), f32[2,32,8,128]{3,2,0,1:T(8,128)S(1)}, u32[]{:S(2)}, u32[]{:S(2)}) %all-to-all-start.15) | async-done | bytes 262176 | tf_op jit(solution)/shard_map/all_to_all | solution.py:159
  167.3 2.8 %all-to-all-start.6 = ((f32[2,32,8,128]{3,2,0,1:T(8,128)}), f32[2,32,8,128]{3,2,0,1:T(8,128)S(1)}, u32[]{:S(2)}, u32[]{:S(2)}) async-start(f32[2,32,8,128]{3,2,0,1:T(8,128)} %copy.147), calls=%async_computation.6 | async-start | bytes 524288 | tf_op jit(solution)/shard_map/all_to_all | solution.py:155
  172.7 7.7 %all-to-all-done.6 = f32[2,32,8,128]{3,2,0,1:T(8,128)S(1)} async-done(((f32[2,32,8,128]{3,2,0,1:T(8,128)}), f32[2,32,8,128]{3,2,0,1:T(8,128)S(1)}, u32[]{:S(2)}, u32[]{:S(2)}) %all-to-all-start.6) | async-done | bytes 262176 | tf_op jit(solution)/shard_map/all_to_all | solution.py:155
  180.4 2.8 %all-to-all-start.12 = ((f32[2,32,8,128]{3,2,0,1:T(8,128)}), f32[2,32,8,128]{3,2,0,1:T(8,128)S(1)}, u32[]{:S(2)}, u32[]{:S(2)}) async-start(f32[2,32,8,128]{3,2,0,1:T(8,128)} %copy.175), calls=%async_computation.12 | async-start | bytes 524288 | tf_op jit(solution)/shard_map/all_to_all | solution.py:157
  184.7 9.0 %all-to-all-done.12 = f32[2,32,8,128]{3,2,0,1:T(8,128)S(1)} async-done(((f32[2,32,8,128]{3,2,0,1:T(8,128)}), f32[2,32,8,128]{3,2,0,1:T(8,128)S(1)}, u32[]{:S(2)}, u32[]{:S(2)}) %all-to-all-start.12) | async-done | bytes 262176 | tf_op jit(solution)/shard_map/all_to_all | solution.py:157
  197.9 8.9 %all-to-all-done.7 = f32[2,32,8,128]{3,2,0,1:T(8,128)S(1)} async-done(((f32[2,32,8,128]{3,2,0,1:T(8,128)}), f32[2,32,8,128]{3,2,0,1:T(8,128)S(1)}, u32[]{:S(2)}, u32[]{:S(2)}) %all-to-all-start.7) | async-done | bytes 262176 | tf_op jit(solution)/shard_map/all_to_all | solution.py:156
  211.1 9.0 %all-to-all-done.13 = f32[2,32,8,128]{3,2,0,1:T(8,128)S(1)} async-done(((f32[2,32,8,128]{3,2,0,1:T(8,128)}), f32[2,32,8,128]{3,2,0,1:T(8,128)S(1)}, u32[]{:S(2)}, u32[]{:S(2)}) %all-to-all-start.13) | async-done | bytes 262176 | tf_op jit(solution)/shard_map/all_to_all | solution.py:158
  225.4 7.6 %all-to-all-done.17 = f32[32,8,128]{2,1,0:T(8,128)S(1)} async-done(((f32[32,8,128]{2,1,0:T(8,128)}), f32[32,8,128]{2,1,0:T(8,128)S(1)}, u32[]{:S(2)}, u32[]{:S(2)}) %all-to-all-start.17) | async-done | bytes 131104 | tf_op jit(solution)/shard_map/all_to_all | solution.py:171
  236.2 7.6 %all-to-all-done.8 = f32[32,8,128]{2,1,0:T(8,128)S(1)} async-done(((f32[32,8,128]{2,1,0:T(8,128)}), f32[32,8,128]{2,1,0:T(8,128)S(1)}, u32[]{:S(2)}, u32[]{:S(2)}) %all-to-all-start.8) | async-done | bytes 131104 | tf_op jit(solution)/shard_map/all_to_all | solution.py:169
  246.3 8.3 %all-to-all-done.14 = f32[32,8,128]{2,1,0:T(8,128)S(1)} async-done(((f32[32,8,128]{2,1,0:T(8,128)}), f32[32,8,128]{2,1,0:T(8,128)S(1)}, u32[]{:S(2)}, u32[]{:S(2)}) %all-to-all-start.14) | async-done | bytes 131104 | tf_op jit(solution)/shard_map/all_to_all | solution.py:170
  (142 shorter events, 80.3 us)
Async XLA Ops:
  0.6 7.1 %copy-start.2 = (f32[256,128]{1,0:T(8,128)S(1)}, f32[256,128]{1,0:T(8,128)}, u32[]{:S(2)}) copy-start(f32[256,128]{1,0:T(8,128)} %param.9) | copy-start | bytes 393220
  0.6 7.1 %copy-start.3 = (f32[256,128]{1,0:T(8,128)S(1)}, f32[256,128]{1,0:T(8,128)}, u32[]{:S(2)}) copy-start(f32[256,128]{1,0:T(8,128)} %param.6) | copy-start | bytes 393220
  0.7 15.3 %all-to-all-start = ((f32[32,8,128]{2,1,0:T(8,128)}), f32[32,8,128]{2,1,0:T(8,128)S(1)}, u32[]{:S(2)}, u32[]{:S(2)}) async-start(f32[32,8,128]{2,1,0:T(8,128)} %bitcast.384), calls=%async_computation | async-start | bytes 262144 | tf_op jit(solution)/shard_map/all_to_all | solution.py:117
  8.5 10.1 %copy-start = (f32[256,128]{1,0:T(8,128)S(1)}, f32[256,128]{1,0:T(8,128)}, u32[]{:S(2)}) copy-start(f32[256,128]{1,0:T(8,128)} %param.8) | copy-start | bytes 393220
  8.5 10.1 %copy-start.1 = (f32[256,128]{1,0:T(8,128)S(1)}, f32[256,128]{1,0:T(8,128)}, u32[]{:S(2)}) copy-start(f32[256,128]{1,0:T(8,128)} %param.7) | copy-start | bytes 393220
  16.0 10.8 %all-to-all-start.9 = ((f32[32,8,128]{2,1,0:T(8,128)}), f32[32,8,128]{2,1,0:T(8,128)S(1)}, u32[]{:S(2)}, u32[]{:S(2)}) async-start(f32[32,8,128]{2,1,0:T(8,128)} %multiply_bitcast_fusion.6), calls=%async_computation.9 | async-start | bytes 262144 | tf_op jit(solution)/shard_map/all_to_all | solution.py:117
  26.8 10.8 %all-to-all-start.3 = ((f32[32,8,128]{2,1,0:T(8,128)}), f32[32,8,128]{2,1,0:T(8,128)S(1)}, u32[]{:S(2)}, u32[]{:S(2)}) async-start(f32[32,8,128]{2,1,0:T(8,128)} %multiply_bitcast_fusion.7), calls=%async_computation.3 | async-start | bytes 262144 | tf_op jit(solution)/shard_map/all_to_all | solution.py:117
  43.8 12.9 %all-to-all-start.10 = ((f32[2,32,8,128]{3,2,0,1:T(8,128)}), f32[2,32,8,128]{3,2,0,1:T(8,128)S(1)}, u32[]{:S(2)}, u32[]{:S(2)}) async-start(f32[2,32,8,128]{3,2,0,1:T(8,128)} %copy.157), calls=%async_computation.10 | async-start | bytes 524288 | tf_op jit(solution)/shard_map/all_to_all | solution.py:135
  56.7 13.2 %all-to-all-start.1 = ((f32[2,32,8,128]{3,2,0,1:T(8,128)}), f32[2,32,8,128]{3,2,0,1:T(8,128)S(1)}, u32[]{:S(2)}, u32[]{:S(2)}) async-start(f32[2,32,8,128]{3,2,0,1:T(8,128)} %copy.109), calls=%async_computation.1 | async-start | bytes 524288 | tf_op jit(solution)/shard_map/all_to_all | solution.py:133
  69.9 13.2 %all-to-all-start.4 = ((f32[2,32,8,128]{3,2,0,1:T(8,128)}), f32[2,32,8,128]{3,2,0,1:T(8,128)S(1)}, u32[]{:S(2)}, u32[]{:S(2)}) async-start(f32[2,32,8,128]{3,2,0,1:T(8,128)} %copy.124), calls=%async_computation.4 | async-start | bytes 524288 | tf_op jit(solution)/shard_map/all_to_all | solution.py:131
  83.1 13.2 %all-to-all-start.11 = ((f32[2,32,8,128]{3,2,0,1:T(8,128)}), f32[2,32,8,128]{3,2,0,1:T(8,128)S(1)}, u32[]{:S(2)}, u32[]{:S(2)}) async-start(f32[2,32,8,128]{3,2,0,1:T(8,128)} %copy.160), calls=%async_computation.11 | async-start | bytes 524288 | tf_op jit(solution)/shard_map/all_to_all | solution.py:136
  96.3 13.2 %all-to-all-start.5 = ((f32[2,32,8,128]{3,2,0,1:T(8,128)}), f32[2,32,8,128]{3,2,0,1:T(8,128)S(1)}, u32[]{:S(2)}, u32[]{:S(2)}) async-start(f32[2,32,8,128]{3,2,0,1:T(8,128)} %copy.127), calls=%async_computation.5 | async-start | bytes 524288 | tf_op jit(solution)/shard_map/all_to_all | solution.py:132
  109.4 13.2 %all-to-all-start.2 = ((f32[2,32,8,128]{3,2,0,1:T(8,128)}), f32[2,32,8,128]{3,2,0,1:T(8,128)S(1)}, u32[]{:S(2)}, u32[]{:S(2)}) async-start(f32[2,32,8,128]{3,2,0,1:T(8,128)} %copy.112), calls=%async_computation.2 | async-start | bytes 524288 | tf_op jit(solution)/shard_map/all_to_all | solution.py:134
  140.9 13.2 %all-to-all-start.16 = ((f32[2,32,8,128]{3,2,0,1:T(8,128)}), f32[2,32,8,128]{3,2,0,1:T(8,128)S(1)}, u32[]{:S(2)}, u32[]{:S(2)}) async-start(f32[2,32,8,128]{3,2,0,1:T(8,128)} %copy.190), calls=%async_computation.16 | async-start | bytes 524288 | tf_op jit(solution)/shard_map/all_to_all | solution.py:160
  154.1 13.2 %all-to-all-start.15 = ((f32[2,32,8,128]{3,2,0,1:T(8,128)}), f32[2,32,8,128]{3,2,0,1:T(8,128)S(1)}, u32[]{:S(2)}, u32[]{:S(2)}) async-start(f32[2,32,8,128]{3,2,0,1:T(8,128)} %copy.188), calls=%async_computation.15 | async-start | bytes 524288 | tf_op jit(solution)/shard_map/all_to_all | solution.py:159
  167.3 13.2 %all-to-all-start.6 = ((f32[2,32,8,128]{3,2,0,1:T(8,128)}), f32[2,32,8,128]{3,2,0,1:T(8,128)S(1)}, u32[]{:S(2)}, u32[]{:S(2)}) async-start(f32[2,32,8,128]{3,2,0,1:T(8,128)} %copy.147), calls=%async_computation.6 | async-start | bytes 524288 | tf_op jit(solution)/shard_map/all_to_all | solution.py:155
  180.4 13.2 %all-to-all-start.12 = ((f32[2,32,8,128]{3,2,0,1:T(8,128)}), f32[2,32,8,128]{3,2,0,1:T(8,128)S(1)}, u32[]{:S(2)}, u32[]{:S(2)}) async-start(f32[2,32,8,128]{3,2,0,1:T(8,128)} %copy.175), calls=%async_computation.12 | async-start | bytes 524288 | tf_op jit(solution)/shard_map/all_to_all | solution.py:157
  193.6 13.2 %all-to-all-start.7 = ((f32[2,32,8,128]{3,2,0,1:T(8,128)}), f32[2,32,8,128]{3,2,0,1:T(8,128)S(1)}, u32[]{:S(2)}, u32[]{:S(2)}) async-start(f32[2,32,8,128]{3,2,0,1:T(8,128)} %copy.149), calls=%async_computation.7 | async-start | bytes 524288 | tf_op jit(solution)/shard_map/all_to_all | solution.py:156
  206.8 13.2 %all-to-all-start.13 = ((f32[2,32,8,128]{3,2,0,1:T(8,128)}), f32[2,32,8,128]{3,2,0,1:T(8,128)S(1)}, u32[]{:S(2)}, u32[]{:S(2)}) async-start(f32[2,32,8,128]{3,2,0,1:T(8,128)} %copy.177), calls=%async_computation.13 | async-start | bytes 524288 | tf_op jit(solution)/shard_map/all_to_all | solution.py:158
  221.9 11.1 %all-to-all-start.17 = ((f32[32,8,128]{2,1,0:T(8,128)}), f32[32,8,128]{2,1,0:T(8,128)S(1)}, u32[]{:S(2)}, u32[]{:S(2)}) async-start(f32[32,8,128]{2,1,0:T(8,128)} %copy.194), calls=%async_computation.17 | async-start | bytes 262144 | tf_op jit(solution)/shard_map/all_to_all | solution.py:171
  233.0 10.8 %all-to-all-start.8 = ((f32[32,8,128]{2,1,0:T(8,128)}), f32[32,8,128]{2,1,0:T(8,128)S(1)}, u32[]{:S(2)}, u32[]{:S(2)}) async-start(f32[32,8,128]{2,1,0:T(8,128)} %copy.153), calls=%async_computation.8 | async-start | bytes 262144 | tf_op jit(solution)/shard_map/all_to_all | solution.py:169
  243.8 10.8 %all-to-all-start.14 = ((f32[32,8,128]{2,1,0:T(8,128)}), f32[32,8,128]{2,1,0:T(8,128)S(1)}, u32[]{:S(2)}, u32[]{:S(2)}) async-start(f32[32,8,128]{2,1,0:T(8,128)} %copy.181), calls=%async_computation.14 | async-start | bytes 262144 | tf_op jit(solution)/shard_map/all_to_all | solution.py:170
  246.3 8.3 %copy-start.4 = (f32[128]{0:T(128)S(1)}, f32[128]{0:T(128)}, u32[]{:S(2)}) copy-start(f32[128]{0:T(128)} %param.11) | copy-start | bytes 1540
where the time goes:
time: 258 us; the launch traced here: 257 us
  waiting for transfers between devices  154 us (60%)
  starting transfers between devices  53 us (21%)
  matrix products  31.3 us (12%)
  local copies, waits for them, and re-layouts  13.3 us (5%)
  other arithmetic  3.79 us (1%)
    dot_general x72, matrix products, apply(): jnp.tensordot(matrix, operand, axes=((1,), (axis,)), precision=highest)  31.3 us
    all_to_all x3, waiting for transfers between devices, local(): lax.all_to_all(blocks, ('sa', 'sb'), split_axis=0, concat_axis=0, tiled=T...  23.3 us
    all_to_all x3, starting transfers between devices, local(): lax.all_to_all(blocks, ('sa', 'sb'), split_axis=0, concat_axis=0, tiled=T...  12 us
    all_to_all x1, waiting for transfers between devices, local(): lax.all_to_all(pending[4], ('sa', 'sb'), split_axis=1, concat_axis=1, til...  9.69 us
    all_to_all x1, waiting for transfers between devices, local(): lax.all_to_all(pending[5], ('sa', 'sb'), split_axis=1, concat_axis=1, til...  9.68 us
    all_to_all x1, waiting for transfers between devices, local(): lax.all_to_all(twisted[4], ('sa', 'sb'), split_axis=1, concat_axis=1, til...  9.55 us
    all_to_all x1, waiting for transfers between devices, local(): lax.all_to_all(twisted[2], ('sa', 'sb'), split_axis=1, concat_axis=1, til...  9.48 us
    all_to_all x1, waiting for transfers between devices, local(): lax.all_to_all(twisted[1], ('sa', 'sb'), split_axis=1, concat_axis=1, til...  9.11 us
  transfers between devices with their start and end apart: 18, of which 18 were waited for; matrix products, arithmetic and copies ran while one was open for 8% of the time, Pallas kernels for 0%

commit v1 on v0

v1 whole, which is shorter than its diff:
```python
import math

import jax
import jax.numpy as jnp
import ml_dtypes
import numpy as np
from jax import lax
from jax.experimental import pallas as pl
from jax.experimental.pallas import tpu as pltpu
from jax.sharding import PartitionSpec as P

LANES = 128
AXES = ("sa", "sb")
VMEM_LIMIT = 48 * 1024 * 1024


def halves(matrix):
    high = matrix.astype(ml_dtypes.bfloat16)
    low = (matrix - high.astype(np.float64)).astype(ml_dtypes.bfloat16)
    return high, low


def tables(tokens, devices):
    rows = tokens // LANES
    parts = rows // devices
    order = np.arange(rows).reshape(devices, parts).T.reshape(-1)
    half_step = np.arange(rows) + 0.5
    lane = np.arange(LANES)
    angle = 2.0 * np.pi / (2 * rows) * half_step[:, None] * order[None, :]
    first = np.concatenate([np.cos(angle), -np.sin(angle)], axis=0)
    turn_angle = 2.0 * np.pi / (2 * tokens) * half_step[:, None] * lane[None, :]
    turn = np.stack([np.cos(turn_angle), -np.sin(turn_angle)]).astype(np.float32)
    lane_angle = 2.0 * np.pi / LANES * ((lane[:, None] * lane[None, :]) % LANES)
    cosine, sine = np.cos(lane_angle), np.sin(lane_angle)
    second = np.block([[cosine, -sine], [sine, cosine]])
    factor = 1.0 / (tokens * math.sqrt(tokens))
    last = np.concatenate([np.cos(angle).T, np.sin(angle).T], axis=1) * factor
    first_high, first_low = halves(first)
    last_high, last_low = halves(last)
    second_high, second_low = halves(second)
    return (
        np.concatenate([first_high, first_high, first_low], axis=1),
        turn,
        np.stack([second_high, second_low]),
        np.concatenate([last_high, last_high, last_low], axis=1),
    )


def split(array):
    scaled = array * 65537.0
    high = scaled - (scaled - array)
    return high, array - high


def stacked(array):
    high, low = split(array)
    return jnp.concatenate([high, low, high], axis=0)


def matmul(left, right):
    return jnp.dot(left, right, preferred_element_type=jnp.float32)


def gate_kernel(devices, *refs):
    far = refs[:6]
    out = refs[6]
    near = refs[7:13]
    arrivals = refs[13]
    copies = [
        pltpu.make_async_copy(source, target, arrivals.at[number])
        for number, (source, target) in enumerate(zip(far, near))
    ]
    for copy in copies:
        copy.start()
    skip, filt, keys, values, cotangent, queries = near
    segment, channels = queries.shape
    parts = segment // LANES
    share = channels // devices
    block = 3 * parts * share
    for number in (1, 0, 2):
        needed = {0: (2, 3), 1: (0, 1), 2: (4, 5)}[number]
        for index in needed:
            copies[index].wait()
        if number == 1:
            first_tap = jnp.where(lax.axis_index(AXES) == 0, math.sqrt(devices * segment), 0.0)
            filt[0:1, :] += first_tap * skip[...]
        for part in range(parts):
            at = pl.ds(part * LANES, LANES)
            if number == 0:
                signal = keys[at, :] * values[at, :]
            elif number == 1:
                signal = filt[at, :]
            else:
                signal = cotangent[at, :] * queries[at, :]
            turned = signal.T
            for channel in range(share):
                row = (number * parts + part) * share + channel
                out[pl.ds(row, devices, stride=block), :] = turned[
                    channel * devices : (channel + 1) * devices, :
                ]


def conv_kernel(devices, arrived, first, turn, second, last, out, high, low):
    rows = turn.shape[1]
    parts = rows // devices
    block = arrived.shape[0] // devices
    share = block // (3 * parts)
    turn_real = turn[0]
    turn_imag = turn[1]

    def gathered(number, channel):
        pieces = []
        for part in range(parts):
            row = (number * parts + part) * share + channel
            pieces.append(arrived[pl.ds(row, devices, stride=block), :])
        return jnp.concatenate(pieces, axis=0)

    def hold(number, channel, real, imag):
        at = pl.ds((channel * 3 + number) * rows, rows)
        for value, lanes in ((real, pl.ds(0, LANES)), (imag, pl.ds(LANES, LANES))):
            high[at, lanes], low[at, lanes] = split(value)

    def lanes_transform(channel):
        at = pl.ds(channel * 3 * rows, 3 * rows)
        result = (
            matmul(high[at, :], second[0])
            + matmul(high[at, :], second[1])
            + matmul(low[at, :], second[0])
        )
        pieces = []
        for number in range(3):
            piece = result[number * rows : (number + 1) * rows]
            pieces.append((piece[:, 0:LANES], piece[:, LANES : 2 * LANES]))
        return pieces

    for number in range(3):
        signals = [stacked(gathered(number, channel)) for channel in range(share)]
        spread = matmul(first[...], jnp.concatenate(signals, axis=1))
        for channel in range(share):
            lanes = slice(channel * LANES, (channel + 1) * LANES)
            real = spread[:rows, lanes]
            imag = spread[rows:, lanes]
            hold(
                number,
                channel,
                real * turn_real - imag * turn_imag,
                real * turn_imag + imag * turn_real,
            )
    for channel in range(share):
        (gr, gi), (fr, fi), (ur, ui) = lanes_transform(channel)
        hold(0, channel, fr * gr - fi * gi, -(fr * gi + fi * gr))
        hold(1, channel, fr * ur + fi * ui, fi * ur - fr * ui)
        hold(2, channel, gr * ur + gi * ui, gi * ur - gr * ui)
    turned = [[], [], []]
    for channel in range(share):
        for number, (real, imag) in enumerate(lanes_transform(channel)):
            both = (real * turn_real - imag * turn_imag, real * turn_imag + imag * turn_real)
            turned[number].append(stacked(jnp.concatenate(both, axis=0)))
    for number in range(3):
        result = matmul(last[...], jnp.concatenate(turned[number], axis=1))
        for channel in range(share):
            lanes = slice(channel * LANES, (channel + 1) * LANES)
            for part in range(parts):
                row = (number * parts + part) * share + channel
                out[pl.ds(row, devices, stride=block), :] = result[
                    part * devices : (part + 1) * devices, lanes
                ]


def finish_kernel(devices, arrived, keys, values, cotangent, *refs):
    far = refs[:4]
    near = refs[4:8]
    departures = refs[8]
    grad_queries, grad_keys, grad_values, grad_filter = near
    segment, channels = keys.shape
    parts = segment // LANES
    share = channels // devices
    block = 3 * parts * share
    copies = [
        pltpu.make_async_copy(source, target, departures.at[number])
        for number, (source, target) in enumerate(zip(near, far))
    ]

    def convolved(number, part):
        pieces = []
        for channel in range(share):
            row = (number * parts + part) * share + channel
            pieces.append(arrived[pl.ds(row, devices, stride=block), :])
        return jnp.concatenate(pieces, axis=0).T

    blocks = [pl.ds(part * LANES, LANES) for part in range(parts)]
    for part, at in enumerate(blocks):
        back_signal = convolved(1, part)
        grad_keys[at, :] = back_signal * values[at, :]
        grad_values[at, :] = back_signal * keys[at, :]
    copies[1].start()
    copies[2].start()
    for part, at in enumerate(blocks):
        grad_queries[at, :] = cotangent[at, :] * convolved(0, part)
    copies[0].start()
    for part, at in enumerate(blocks):
        grad_filter[at, :] = convolved(2, part)
    copies[3].start()
    for copy in copies:
        copy.wait()


def call(kernel, devices, out_shape, scratch=(), **specs):
    def bound(*refs):
        kernel(devices, *refs)

    return pl.pallas_call(
        bound,
        out_shape=out_shape,
        scratch_shapes=scratch,
        compiler_params=pltpu.CompilerParams(vmem_limit_bytes=VMEM_LIMIT),
        **specs,
    )


def local(queries, keys, values, cotangent, filt, skip):
    segment, channels = queries.shape
    devices = lax.axis_size(AXES)
    tokens = segment * devices
    rows = tokens // LANES
    share = channels // devices
    block = 3 * (segment // LANES) * share
    flat = pltpu.VMEM((devices * block, LANES), jnp.float32)

    def exchange(array):
        array = array.reshape(devices, block, LANES)
        array = lax.all_to_all(array, AXES, split_axis=0, concat_axis=0, tiled=True)
        return array.reshape(devices * block, LANES)

    whole = pltpu.VMEM((segment, channels), jnp.float32)
    result = jax.ShapeDtypeStruct(whole.shape, whole.dtype)
    far = pl.BlockSpec(memory_space=pltpu.HBM)
    near = pl.BlockSpec(memory_space=pltpu.VMEM)
    operands = (skip.reshape(1, channels), filt, keys, values, cotangent, queries)
    operands = tuple(pltpu.with_memory_space_constraint(array, pltpu.HBM) for array in operands)
    scratch = (pltpu.VMEM((1, channels), jnp.float32),) + (whole,) * 5 + (pltpu.SemaphoreType.DMA((6,)),)
    gate = call(gate_kernel, devices, flat, scratch, in_specs=(far,) * 6)
    arrived = exchange(gate(*operands))
    wide = pltpu.VMEM((3 * share * rows, 2 * LANES), jnp.float32)
    constants = tuple(jnp.asarray(table, jnp.float32) for table in tables(tokens, devices))
    convolved = call(conv_kernel, devices, flat, (wide, wide))(arrived, *constants)
    returned = exchange(convolved)
    finish = call(
        finish_kernel,
        devices,
        (result,) * 4,
        (whole,) * 4 + (pltpu.SemaphoreType.DMA((4,)),),
        in_specs=(near,) * 4,
        out_specs=(far,) * 4,
    )
    return tuple(finish(returned, keys, values, cotangent))


def solution(mesh):
    whole = P(AXES, None)
    return jax.shard_map(
        local,
        mesh=mesh,
        in_specs=(whole,) * 5 + (P(),),
        out_specs=(whole,) * 4,
        check_vma=False,
    )
```

time: 258 us -> 40.5 us (0.16)
  the two profiles are of different devices: /device:TPU:1 before, /device:TPU:0 now
where the time goes in v1:
time: 40.5 us; the launch traced here: 40.3 us
  blocking collectives  35.9 us (89%)
  Pallas kernels  3.6 us (9%)
  between operations  0.72 us (2%)
    all_to_all x2, blocking collectives, exchange(): array = lax.all_to_all(array, AXES, split_axis=0, concat_axis=0, tiled=True)  35.9 us
    pallas_call x1, Pallas kernels, local(): arrived = exchange(gate(*operands))  1.36 us
    pallas_call x1, Pallas kernels, local(): call(conv_kernel, devices, flat, (wide, wide))(arrived, *constants)  1.31 us
    pallas_call x1, Pallas kernels, local(): return tuple(finish(returned, keys, values, cotangent))  0.92 us

profile of v1, /device:TPU:0, one launch (start us, length us, event | category | flops | bytes accessed | tf_op | source)
XLA Modules:
  0.0 40.3 jit_solution(14716700355279490503)
XLA Ops:
  0.6 0.0 copy-start.6
  0.6 1.4 %shard_map.129 = f32[768,128]{1,0:T(8,128)S(1)} custom-call(f32[1,128]{1,0:T(1,128)} %bitcast.9, f32[256,128]{1,0:T(8,128)} %refs_1_.3, f32[256,128]{1,0:T(8,128)} %refs_1_.4, f32[256,128]{1,0:T(8,128)} %refs_2_.4, f32[256,128]{1,0:T(8,128)} %refs_3_.4, f32[256,128]{1,0:T(8,128)} %refs_5_.1), custom_call_target="tpu_custom_call" | custom-call | tf_op jit(solution)/shard_map/pallas_call | solution.py:243
  2.0 0.0 copy-start
  2.0 0.0 copy-start.4
  2.0 0.0 copy-start.5
  2.0 20.3 %all_to_all.10 = f32[32,24,128]{2,1,0:T(8,128)S(1)} all-to-all(f32[32,24,128]{2,1,0:T(8,128)S(1)} %bitcast.8), channel_id=1, replica_groups=mesh['sa'=4,'sb'=8] {'sa','sb'}, dimensions={0} | all-to-all | bytes 786432 | tf_op jit(solution)/shard_map/all_to_all | solution.py:232
  22.3 0.0 copy-done.6
  22.3 0.0 copy-done
  22.3 0.0 copy-done.4
  22.3 0.0 copy-done.5
  22.4 1.3 %shard_map.130 = f32[768,128]{1,0:T(8,128)S(1)} custom-call(f32[768,128]{1,0:T(8,128)S(1)} %bitcast.6, f32[128,192]{1,0:T(8,128)S(1)} %copy-done.4, f32[2,64,128]{2,1,0:T(8,128)S(1)} %copy-done.6, f32[2,256,256]{2,1,0:T(8,128)S(1)} %copy-done, f32[64,384]{1,0:T(8,128)S(1)} %copy-done.5), custom_call_target="tpu_custom_call" | custom-call | tf_op jit(solution)/shard_map/pallas_call | solution.py:246
  23.7 0.0 copy-start.1
  23.7 0.0 copy-start.2
  23.7 0.0 copy-start.3
  23.7 15.6 %all_to_all.11 = f32[32,24,128]{2,1,0:T(8,128)S(1)} all-to-all(f32[32,24,128]{2,1,0:T(8,128)S(1)} %bitcast.7), channel_id=1, replica_groups=mesh['sa'=4,'sb'=8] {'sa','sb'}, dimensions={0} | all-to-all | bytes 786432 | tf_op jit(solution)/shard_map/all_to_all | solution.py:232
  39.3 0.0 copy-done.1
  39.3 0.0 copy-done.2
  39.3 0.0 copy-done.3
  39.3 0.9 %shard_map.131 = (f32[256,128]{1,0:T(8,128)}, f32[256,128]{1,0:T(8,128)}, f32[256,128]{1,0:T(8,128)}, f32[256,128]{1,0:T(8,128)}) custom-call(f32[768,128]{1,0:T(8,128)S(1)} %bitcast.5, f32[256,128]{1,0:T(8,128)S(1)} %copy-done.1, f32[256,128]{1,0:T(8,128)S(1)} %copy-done.2, f32[256,128]{1,0:T(8,128)S(1)} %copy-done.3), custom_call_target="tpu_custom_call" | custom-call | tf_op jit(solution)/shard_map/pallas_call | solution.py:256
Async XLA Ops:
  0.6 21.7 %copy-start.6 = (f32[2,64,128]{2,1,0:T(8,128)S(1)}, f32[2,64,128]{2,1,0:T(8,128)}, u32[]{:S(2)}) copy-start(f32[2,64,128]{2,1,0:T(8,128)} %constant.9.clone.refs_2_) | copy-start | bytes 196612
  2.0 20.3 %copy-start = (f32[2,256,256]{2,1,0:T(8,128)S(1)}, f32[2,256,256]{2,1,0:T(8,128)}, u32[]{:S(2)}) copy-start(f32[2,256,256]{2,1,0:T(8,128)} %constant.10.clone.refs_3_) | copy-start | bytes 1572868
  2.0 20.3 %copy-start.4 = (f32[128,192]{1,0:T(8,128)S(1)}, f32[128,192]{1,0:T(8,128)}, u32[]{:S(2)}) copy-start(f32[128,192]{1,0:T(8,128)} %constant.8.clone.refs_1_) | copy-start | bytes 294916
  2.0 20.3 %copy-start.5 = (f32[64,384]{1,0:T(8,128)S(1)}, f32[64,384]{1,0:T(8,128)}, u32[]{:S(2)}) copy-start(f32[64,384]{1,0:T(8,128)} %constant.11.clone.refs_4_) | copy-start | bytes 294916
  23.7 15.7 %copy-start.1 = (f32[256,128]{1,0:T(8,128)S(1)}, f32[256,128]{1,0:T(8,128)}, u32[]{:S(2)}) copy-start(f32[256,128]{1,0:T(8,128)} %refs_1_.4) | copy-start | bytes 393220
  23.7 15.6 %copy-start.2 = (f32[256,128]{1,0:T(8,128)S(1)}, f32[256,128]{1,0:T(8,128)}, u32[]{:S(2)}) copy-start(f32[256,128]{1,0:T(8,128)} %refs_2_.4) | copy-start | bytes 393220
  23.7 15.6 %copy-start.3 = (f32[256,128]{1,0:T(8,128)S(1)}, f32[256,128]{1,0:T(8,128)}, u32[]{:S(2)}) copy-start(f32[256,128]{1,0:T(8,128)} %refs_3_.4) | copy-start | bytes 393220

commit v2 on v1

--- a/solution.py
+++ b/solution.py
@@ -11,6 +11,7 @@
 
 LANES = 128
 AXES = ("sa", "sb")
+EXCHANGE = ("sb", "sa")
 VMEM_LIMIT = 48 * 1024 * 1024
 
 
@@ -20,10 +21,10 @@
     return high, low
 
 
-def tables(tokens, devices):
+def tables(tokens, devices, planes):
     rows = tokens // LANES
     parts = rows // devices
-    order = np.arange(rows).reshape(devices, parts).T.reshape(-1)
+    order = np.arange(rows).reshape(planes, devices // planes, parts).transpose(2, 1, 0).reshape(-1)
     half_step = np.arange(rows) + 0.5
     lane = np.arange(LANES)
     angle = 2.0 * np.pi / (2 * rows) * half_step[:, None] * order[None, :]
@@ -47,9 +48,9 @@
 
 
 def split(array):
-    scaled = array * 65537.0
-    high = scaled - (scaled - array)
-    return high, array - high
+    high = array.astype(jnp.bfloat16)
+    low = (array - high.astype(jnp.float32)).astype(jnp.bfloat16)
+    return high, low
 
 
 def stacked(array):
@@ -229,7 +230,7 @@
 
     def exchange(array):
         array = array.reshape(devices, block, LANES)
-        array = lax.all_to_all(array, AXES, split_axis=0, concat_axis=0, tiled=True)
+        array = lax.all_to_all(array, EXCHANGE, split_axis=0, concat_axis=0, tiled=True)
         return array.reshape(devices * block, LANES)
 
     whole = pltpu.VMEM((segment, channels), jnp.float32)
@@ -241,8 +242,8 @@
     scratch = (pltpu.VMEM((1, channels), jnp.float32),) + (whole,) * 5 + (pltpu.SemaphoreType.DMA((6,)),)
     gate = call(gate_kernel, devices, flat, scratch, in_specs=(far,) * 6)
     arrived = exchange(gate(*operands))
-    wide = pltpu.VMEM((3 * share * rows, 2 * LANES), jnp.float32)
-    constants = tuple(jnp.asarray(table, jnp.float32) for table in tables(tokens, devices))
+    wide = pltpu.VMEM((3 * share * rows, 2 * LANES), jnp.bfloat16)
+    constants = tuple(jnp.asarray(table) for table in tables(tokens, devices, lax.axis_size(AXES[0])))
     convolved = call(conv_kernel, devices, flat, (wide, wide))(arrived, *constants)
     returned = exchange(convolved)
     finish = call(

time: 40.5 us -> 39.7 us (0.980)
  the two profiles are of different devices: /device:TPU:0 before, /device:TPU:1 now
where the time goes in v2:
time: 39.7 us; the launch traced here: 39.5 us
  blocking collectives  35.1 us (88%)
  Pallas kernels  3.59 us (9%)
  between operations  0.72 us (2%)
    all_to_all x2, blocking collectives, exchange(): lax.all_to_all(array, EXCHANGE, split_axis=0, concat_axis=0, tiled=True)  35.1 us
    pallas_call x1, Pallas kernels, local(): call(conv_kernel, devices, flat, (wide, wide))(arrived, *constants)  1.34 us
    pallas_call x1, Pallas kernels, local(): arrived = exchange(gate(*operands))  1.33 us
    pallas_call x1, Pallas kernels, local(): return tuple(finish(returned, keys, values, cotangent))  0.92 us

profile of v2, /device:TPU:1, one launch (start us, length us, event | category | flops | bytes accessed | tf_op | source)
XLA Modules:
  0.0 39.5 jit_solution(3132206793089974060)
XLA Ops:
  0.6 1.3 %shard_map.129 = f32[768,128]{1,0:T(8,128)S(1)} custom-call(f32[1,128]{1,0:T(1,128)} %bitcast.9, f32[256,128]{1,0:T(8,128)} %refs_1_.3, f32[256,128]{1,0:T(8,128)} %refs_1_.4, f32[256,128]{1,0:T(8,128)} %refs_2_.4, f32[256,128]{1,0:T(8,128)} %refs_3_.4, f32[256,128]{1,0:T(8,128)} %refs_5_.1), custom_call_target="tpu_custom_call" | custom-call | tf_op jit(solution)/shard_map/pallas_call | solution.py:244
  2.0 0.0 copy-start.3
  2.0 0.0 copy-start.4
  2.0 0.0 copy-start.5
  2.0 0.0 copy-start.6
  2.0 19.6 %all_to_all.10 = f32[32,24,128]{2,1,0:T(8,128)S(1)} all-to-all(f32[32,24,128]{2,1,0:T(8,128)S(1)} %bitcast.8), channel_id=1, replica_groups=mesh['sa'=4,'sb'=8] {'sb','sa'}, dimensions={0} | all-to-all | bytes 786432 | tf_op jit(solution)/shard_map/all_to_all | solution.py:233
  21.7 0.0 copy-done.3
  21.7 0.0 copy-done.4
  21.7 0.0 copy-done.5
  21.7 0.0 copy-done.6
  21.7 1.3 %shard_map.130 = f32[768,128]{1,0:T(8,128)S(1)} custom-call(f32[768,128]{1,0:T(8,128)S(1)} %bitcast.6, bf16[128,192]{1,0:T(8,128)(2,1)S(1)} %copy-done.5, f32[2,64,128]{2,1,0:T(8,128)S(1)} %copy-done.4, bf16[2,256,256]{2,1,0:T(8,128)(2,1)S(1)} %copy-done.3, bf16[64,384]{1,0:T(8,128)(2,1)S(1)} %copy-done.6), custom_call_target="tpu_custom_call" | custom-call | tf_op jit(solution)/shard_map/pallas_call | solution.py:247
  23.0 0.0 copy-start
  23.1 0.0 copy-start.1
  23.1 0.0 copy-start.2
  23.1 15.5 %all_to_all.11 = f32[32,24,128]{2,1,0:T(8,128)S(1)} all-to-all(f32[32,24,128]{2,1,0:T(8,128)S(1)} %bitcast.7), channel_id=1, replica_groups=mesh['sa'=4,'sb'=8] {'sb','sa'}, dimensions={0} | all-to-all | bytes 786432 | tf_op jit(solution)/shard_map/all_to_all | solution.py:233
  38.6 0.0 copy-done
  38.6 0.0 copy-done.1
  38.6 0.0 copy-done.2
  38.6 0.9 %shard_map.131 = (f32[256,128]{1,0:T(8,128)}, f32[256,128]{1,0:T(8,128)}, f32[256,128]{1,0:T(8,128)}, f32[256,128]{1,0:T(8,128)}) custom-call(f32[768,128]{1,0:T(8,128)S(1)} %bitcast.5, f32[256,128]{1,0:T(8,128)S(1)} %copy-done, f32[256,128]{1,0:T(8,128)S(1)} %copy-done.1, f32[256,128]{1,0:T(8,128)S(1)} %copy-done.2), custom_call_target="tpu_custom_call" | custom-call | tf_op jit(solution)/shard_map/pallas_call | solution.py:257
Async XLA Ops:
  2.0 19.7 %copy-start.3 = (bf16[2,256,256]{2,1,0:T(8,128)(2,1)S(1)}, bf16[2,256,256]{2,1,0:T(8,128)(2,1)}, u32[]{:S(2)}) copy-start(bf16[2,256,256]{2,1,0:T(8,128)(2,1)} %constant.10.clone.refs_3_) | copy-start | bytes 786436
  2.0 19.7 %copy-start.4 = (f32[2,64,128]{2,1,0:T(8,128)S(1)}, f32[2,64,128]{2,1,0:T(8,128)}, u32[]{:S(2)}) copy-start(f32[2,64,128]{2,1,0:T(8,128)} %constant.9.clone.refs_2_) | copy-start | bytes 196612
  2.0 19.7 %copy-start.5 = (bf16[128,192]{1,0:T(8,128)(2,1)S(1)}, bf16[128,192]{1,0:T(8,128)(2,1)}, u32[]{:S(2)}) copy-start(bf16[128,192]{1,0:T(8,128)(2,1)} %constant.8.clone.refs_1_) | copy-start | bytes 147460
  2.0 19.7 %copy-start.6 = (bf16[64,384]{1,0:T(8,128)(2,1)S(1)}, bf16[64,384]{1,0:T(8,128)(2,1)}, u32[]{:S(2)}) copy-start(bf16[64,384]{1,0:T(8,128)(2,1)} %constant.11.clone.refs_4_) | copy-start | bytes 147460
  23.0 15.5 %copy-start = (f32[256,128]{1,0:T(8,128)S(1)}, f32[256,128]{1,0:T(8,128)}, u32[]{:S(2)}) copy-start(f32[256,128]{1,0:T(8,128)} %refs_1_.4) | copy-start | bytes 393220
  23.1 15.5 %copy-start.1 = (f32[256,128]{1,0:T(8,128)S(1)}, f32[256,128]{1,0:T(8,128)}, u32[]{:S(2)}) copy-start(f32[256,128]{1,0:T(8,128)} %refs_2_.4) | copy-start | bytes 393220
  23.1 15.5 %copy-start.2 = (f32[256,128]{1,0:T(8,128)S(1)}, f32[256,128]{1,0:T(8,128)}, u32[]{:S(2)}) copy-start(f32[256,128]{1,0:T(8,128)} %refs_3_.4) | copy-start | bytes 393220

commit v3 on v2

--- a/solution.py
+++ b/solution.py
@@ -11,7 +11,6 @@
 
 LANES = 128
 AXES = ("sa", "sb")
-EXCHANGE = ("sb", "sa")
 VMEM_LIMIT = 48 * 1024 * 1024
 
 
@@ -21,10 +20,14 @@
     return high, low
 
 
-def tables(tokens, devices, planes):
+def exchange_order(planes, width):
+    return [plane * width + place for place in range(width) for plane in reversed(range(planes))]
+
+
+def tables(tokens, devices, group):
     rows = tokens // LANES
     parts = rows // devices
-    order = np.arange(rows).reshape(planes, devices // planes, parts).transpose(2, 1, 0).reshape(-1)
+    order = (np.array(group)[None, :] * parts + np.arange(parts)[:, None]).reshape(-1)
     half_step = np.arange(rows) + 0.5
     lane = np.arange(LANES)
     angle = 2.0 * np.pi / (2 * rows) * half_step[:, None] * order[None, :]
@@ -228,9 +231,12 @@
     block = 3 * (segment // LANES) * share
     flat = pltpu.VMEM((devices * block, LANES), jnp.float32)
 
+    group = exchange_order(lax.axis_size(AXES[0]), lax.axis_size(AXES[1]))
+
     def exchange(array):
-        array = array.reshape(devices, block, LANES)
-        array = lax.all_to_all(array, EXCHANGE, split_axis=0, concat_axis=0, tiled=True)
+        array = lax.all_to_all(
+            array, AXES, split_axis=0, concat_axis=0, axis_index_groups=[group], tiled=True
+        )
         return array.reshape(devices * block, LANES)
 
     whole = pltpu.VMEM((segment, channels), jnp.float32)
@@ -243,7 +249,7 @@
     gate = call(gate_kernel, devices, flat, scratch, in_specs=(far,) * 6)
     arrived = exchange(gate(*operands))
     wide = pltpu.VMEM((3 * share * rows, 2 * LANES), jnp.bfloat16)
-    constants = tuple(jnp.asarray(table) for table in tables(tokens, devices, lax.axis_size(AXES[0])))
+    constants = tuple(jnp.asarray(table) for table in tables(tokens, devices, group))
     convolved = call(conv_kernel, devices, flat, (wide, wide))(arrived, *constants)
     returned = exchange(convolved)
     finish = call(

time: 39.7 us -> 39.9 us (level)
  the two profiles are of different devices: /device:TPU:1 before, /device:TPU:0 now
where the time goes in v3:
time: 39.9 us; the launch traced here: 39.7 us
  blocking collectives  35.4 us (89%)
  Pallas kernels  3.6 us (9%)
  between operations  0.72 us (2%)
    all_to_all x2, blocking collectives, exchange(): lax.all_to_all(array, AXES, split_axis=0, concat_axis=0, axis_index_group...  35.4 us
    pallas_call x1, Pallas kernels, local(): call(conv_kernel, devices, flat, (wide, wide))(arrived, *constants)  1.34 us
    pallas_call x1, Pallas kernels, local(): arrived = exchange(gate(*operands))  1.33 us
    pallas_call x1, Pallas kernels, local(): return tuple(finish(returned, keys, values, cotangent))  0.92 us

profile of v3, /device:TPU:0, one launch (start us, length us, event | category | flops | bytes accessed | tf_op | source)
XLA Modules:
  0.0 39.7 jit_solution(7303181563634726860)
XLA Ops:
  0.6 1.3 %shard_map.129 = f32[768,128]{1,0:T(8,128)S(1)} custom-call(f32[1,128]{1,0:T(1,128)} %bitcast.9, f32[256,128]{1,0:T(8,128)} %refs_1_.3, f32[256,128]{1,0:T(8,128)} %refs_1_.4, f32[256,128]{1,0:T(8,128)} %refs_2_.4, f32[256,128]{1,0:T(8,128)} %refs_3_.4, f32[256,128]{1,0:T(8,128)} %refs_5_.1), custom_call_target="tpu_custom_call" | custom-call | tf_op jit(solution)/shard_map/pallas_call | solution.py:250
  2.0 0.0 copy-start.3
  2.0 0.0 copy-start.4
  2.0 0.0 copy-start.5
  2.0 0.0 copy-start.6
  2.0 20.3 %all_to_all.22 = f32[32,24,128]{2,1,0:T(8,128)S(1)} all-to-all(f32[32,24,128]{2,1,0:T(8,128)S(1)} %bitcast.8), channel_id=1, replica_groups={{24,16,8,0,25,17,9,1,26,18,10,2,27,19,11,3,28,20,12,4,29,21,13,5,30,22,..., dimensions={0} | all-to-all | bytes 786432 | tf_op jit(solution)/shard_map/all_to_all | solution.py:237
  22.3 0.0 copy-done.3
  22.3 0.0 copy-done.4
  22.3 0.0 copy-done.5
  22.3 0.0 copy-done.6
  22.3 1.3 %shard_map.130 = f32[768,128]{1,0:T(8,128)S(1)} custom-call(f32[768,128]{1,0:T(8,128)S(1)} %bitcast.6, bf16[128,192]{1,0:T(8,128)(2,1)S(1)} %copy-done.5, f32[2,64,128]{2,1,0:T(8,128)S(1)} %copy-done.4, bf16[2,256,256]{2,1,0:T(8,128)(2,1)S(1)} %copy-done.3, bf16[64,384]{1,0:T(8,128)(2,1)S(1)} %copy-done.6), custom_call_target="tpu_custom_call" | custom-call | tf_op jit(solution)/shard_map/pallas_call | solution.py:253
  23.7 0.0 copy-start
  23.7 0.0 copy-start.1
  23.7 0.0 copy-start.2
  23.7 15.1 %all_to_all.23 = f32[32,24,128]{2,1,0:T(8,128)S(1)} all-to-all(f32[32,24,128]{2,1,0:T(8,128)S(1)} %bitcast.7), channel_id=1, replica_groups={{24,16,8,0,25,17,9,1,26,18,10,2,27,19,11,3,28,20,12,4,29,21,13,5,30,22,..., dimensions={0} | all-to-all | bytes 786432 | tf_op jit(solution)/shard_map/all_to_all | solution.py:237
  38.8 0.0 copy-done
  38.8 0.0 copy-done.1
  38.8 0.0 copy-done.2
  38.8 0.9 %shard_map.131 = (f32[256,128]{1,0:T(8,128)}, f32[256,128]{1,0:T(8,128)}, f32[256,128]{1,0:T(8,128)}, f32[256,128]{1,0:T(8,128)}) custom-call(f32[768,128]{1,0:T(8,128)S(1)} %bitcast.5, f32[256,128]{1,0:T(8,128)S(1)} %copy-done, f32[256,128]{1,0:T(8,128)S(1)} %copy-done.1, f32[256,128]{1,0:T(8,128)S(1)} %copy-done.2), custom_call_target="tpu_custom_call" | custom-call | tf_op jit(solution)/shard_map/pallas_call | solution.py:263
Async XLA Ops:
  2.0 20.3 %copy-start.3 = (bf16[2,256,256]{2,1,0:T(8,128)(2,1)S(1)}, bf16[2,256,256]{2,1,0:T(8,128)(2,1)}, u32[]{:S(2)}) copy-start(bf16[2,256,256]{2,1,0:T(8,128)(2,1)} %constant.10.clone.refs_3_) | copy-start | bytes 786436
  2.0 20.3 %copy-start.4 = (f32[2,64,128]{2,1,0:T(8,128)S(1)}, f32[2,64,128]{2,1,0:T(8,128)}, u32[]{:S(2)}) copy-start(f32[2,64,128]{2,1,0:T(8,128)} %constant.9.clone.refs_2_) | copy-start | bytes 196612
  2.0 20.3 %copy-start.5 = (bf16[128,192]{1,0:T(8,128)(2,1)S(1)}, bf16[128,192]{1,0:T(8,128)(2,1)}, u32[]{:S(2)}) copy-start(bf16[128,192]{1,0:T(8,128)(2,1)} %constant.8.clone.refs_1_) | copy-start | bytes 147460
  2.0 20.3 %copy-start.6 = (bf16[64,384]{1,0:T(8,128)(2,1)S(1)}, bf16[64,384]{1,0:T(8,128)(2,1)}, u32[]{:S(2)}) copy-start(bf16[64,384]{1,0:T(8,128)(2,1)} %constant.11.clone.refs_4_) | copy-start | bytes 147460
  23.7 15.1 %copy-start = (f32[256,128]{1,0:T(8,128)S(1)}, f32[256,128]{1,0:T(8,128)}, u32[]{:S(2)}) copy-start(f32[256,128]{1,0:T(8,128)} %refs_1_.4) | copy-start | bytes 393220
  23.7 15.1 %copy-start.1 = (f32[256,128]{1,0:T(8,128)S(1)}, f32[256,128]{1,0:T(8,128)}, u32[]{:S(2)}) copy-start(f32[256,128]{1,0:T(8,128)} %refs_2_.4) | copy-start | bytes 393220
  23.7 15.1 %copy-start.2 = (f32[256,128]{1,0:T(8,128)S(1)}, f32[256,128]{1,0:T(8,128)}, u32[]{:S(2)}) copy-start(f32[256,128]{1,0:T(8,128)} %refs_3_.4) | copy-start | bytes 393220

commit v4 on v3

--- a/solution.py
+++ b/solution.py
@@ -21,7 +21,9 @@
 
 
 def exchange_order(planes, width):
-    return [plane * width + place for place in range(width) for plane in reversed(range(planes))]
+    lower = planes // 2
+    turns = [plane for pair in zip(range(lower), range(lower, planes)) for plane in pair]
+    return [plane * width + place for place in range(width) for plane in reversed(turns)]
 
 
 def tables(tokens, devices, group):

time: 39.9 us -> 40.3 us (1.010)
  the two profiles are of different devices: /device:TPU:0 before, /device:TPU:1 now
where the time goes in v4:
time: 40.3 us; the launch traced here: 40.1 us
  blocking collectives  35.7 us (89%)
  Pallas kernels  3.59 us (9%)
  between operations  0.72 us (2%)
    all_to_all x2, blocking collectives, exchange(): lax.all_to_all(array, AXES, split_axis=0, concat_axis=0, axis_index_group...  35.7 us
    pallas_call x1, Pallas kernels, local(): call(conv_kernel, devices, flat, (wide, wide))(arrived, *constants)  1.34 us
    pallas_call x1, Pallas kernels, local(): arrived = exchange(gate(*operands))  1.33 us
    pallas_call x1, Pallas kernels, local(): return tuple(finish(returned, keys, values, cotangent))  0.92 us

profile of v4, /device:TPU:1, one launch (start us, length us, event | category | flops | bytes accessed | tf_op | source)
XLA Modules:
  0.0 40.1 jit_solution(11591099695393617032)
XLA Ops:
  0.6 1.3 %shard_map.129 = f32[768,128]{1,0:T(8,128)S(1)} custom-call(f32[1,128]{1,0:T(1,128)} %bitcast.9, f32[256,128]{1,0:T(8,128)} %refs_1_.3, f32[256,128]{1,0:T(8,128)} %refs_1_.4, f32[256,128]{1,0:T(8,128)} %refs_2_.4, f32[256,128]{1,0:T(8,128)} %refs_3_.4, f32[256,128]{1,0:T(8,128)} %refs_5_.1), custom_call_target="tpu_custom_call" | custom-call | tf_op jit(solution)/shard_map/pallas_call | solution.py:252
  2.0 0.0 copy-start.3
  2.0 0.0 copy-start.4
  2.0 0.0 copy-start.5
  2.0 0.0 copy-start.6
  2.0 20.2 %all_to_all.22 = f32[32,24,128]{2,1,0:T(8,128)S(1)} all-to-all(f32[32,24,128]{2,1,0:T(8,128)S(1)} %bitcast.8), channel_id=1, replica_groups={{24,8,16,0,25,9,17,1,26,10,18,2,27,11,19,3,28,12,20,4,29,13,21,5,30,14,..., dimensions={0} | all-to-all | bytes 786432 | tf_op jit(solution)/shard_map/all_to_all | solution.py:239
  22.3 0.0 copy-done.3
  22.3 0.0 copy-done.4
  22.3 0.0 copy-done.5
  22.3 0.0 copy-done.6
  22.3 1.3 %shard_map.130 = f32[768,128]{1,0:T(8,128)S(1)} custom-call(f32[768,128]{1,0:T(8,128)S(1)} %bitcast.6, bf16[128,192]{1,0:T(8,128)(2,1)S(1)} %copy-done.5, f32[2,64,128]{2,1,0:T(8,128)S(1)} %copy-done.4, bf16[2,256,256]{2,1,0:T(8,128)(2,1)S(1)} %copy-done.3, bf16[64,384]{1,0:T(8,128)(2,1)S(1)} %copy-done.6), custom_call_target="tpu_custom_call" | custom-call | tf_op jit(solution)/shard_map/pallas_call | solution.py:255
  23.6 0.0 copy-start
  23.6 0.0 copy-start.1
  23.6 0.0 copy-start.2
  23.7 15.5 %all_to_all.23 = f32[32,24,128]{2,1,0:T(8,128)S(1)} all-to-all(f32[32,24,128]{2,1,0:T(8,128)S(1)} %bitcast.7), channel_id=1, replica_groups={{24,8,16,0,25,9,17,1,26,10,18,2,27,11,19,3,28,12,20,4,29,13,21,5,30,14,..., dimensions={0} | all-to-all | bytes 786432 | tf_op jit(solution)/shard_map/all_to_all | solution.py:239
  39.1 0.0 copy-done
  39.2 0.0 copy-done.1
  39.2 0.0 copy-done.2
  39.2 0.9 %shard_map.131 = (f32[256,128]{1,0:T(8,128)}, f32[256,128]{1,0:T(8,128)}, f32[256,128]{1,0:T(8,128)}, f32[256,128]{1,0:T(8,128)}) custom-call(f32[768,128]{1,0:T(8,128)S(1)} %bitcast.5, f32[256,128]{1,0:T(8,128)S(1)} %copy-done, f32[256,128]{1,0:T(8,128)S(1)} %copy-done.1, f32[256,128]{1,0:T(8,128)S(1)} %copy-done.2), custom_call_target="tpu_custom_call" | custom-call | tf_op jit(solution)/shard_map/pallas_call | solution.py:265
Async XLA Ops:
  2.0 20.3 %copy-start.3 = (bf16[2,256,256]{2,1,0:T(8,128)(2,1)S(1)}, bf16[2,256,256]{2,1,0:T(8,128)(2,1)}, u32[]{:S(2)}) copy-start(bf16[2,256,256]{2,1,0:T(8,128)(2,1)} %constant.10.clone.refs_3_) | copy-start | bytes 786436
  2.0 20.3 %copy-start.4 = (f32[2,64,128]{2,1,0:T(8,128)S(1)}, f32[2,64,128]{2,1,0:T(8,128)}, u32[]{:S(2)}) copy-start(f32[2,64,128]{2,1,0:T(8,128)} %constant.9.clone.refs_2_) | copy-start | bytes 196612
  2.0 20.3 %copy-start.5 = (bf16[128,192]{1,0:T(8,128)(2,1)S(1)}, bf16[128,192]{1,0:T(8,128)(2,1)}, u32[]{:S(2)}) copy-start(bf16[128,192]{1,0:T(8,128)(2,1)} %constant.8.clone.refs_1_) | copy-start | bytes 147460
  2.0 20.3 %copy-start.6 = (bf16[64,384]{1,0:T(8,128)(2,1)S(1)}, bf16[64,384]{1,0:T(8,128)(2,1)}, u32[]{:S(2)}) copy-start(bf16[64,384]{1,0:T(8,128)(2,1)} %constant.11.clone.refs_4_) | copy-start | bytes 147460
  23.6 15.5 %copy-start = (f32[256,128]{1,0:T(8,128)S(1)}, f32[256,128]{1,0:T(8,128)}, u32[]{:S(2)}) copy-start(f32[256,128]{1,0:T(8,128)} %refs_1_.4) | copy-start | bytes 393220
  23.6 15.5 %copy-start.1 = (f32[256,128]{1,0:T(8,128)S(1)}, f32[256,128]{1,0:T(8,128)}, u32[]{:S(2)}) copy-start(f32[256,128]{1,0:T(8,128)} %refs_2_.4) | copy-start | bytes 393220
  23.6 15.5 %copy-start.2 = (f32[256,128]{1,0:T(8,128)S(1)}, f32[256,128]{1,0:T(8,128)}, u32[]{:S(2)}) copy-start(f32[256,128]{1,0:T(8,128)} %refs_3_.4) | copy-start | bytes 393220

commit v5 on v3

--- a/solution.py
+++ b/solution.py
@@ -21,7 +21,7 @@
 
 
 def exchange_order(planes, width):
-    return [plane * width + place for place in range(width) for plane in reversed(range(planes))]
+    return [-plane % planes * width + place for place in range(width) for plane in range(planes)]
 
 
 def tables(tokens, devices, group):

time: 39.9 us -> 39.3 us (0.985)
  the two profiles are of different devices: /device:TPU:0 before, /device:TPU:1 now
where the time goes in v5:
time: 39.3 us; the launch traced here: 39.1 us
  blocking collectives  34.7 us (88%)
  Pallas kernels  3.59 us (9%)
  between operations  0.72 us (2%)
    all_to_all x2, blocking collectives, exchange(): lax.all_to_all(array, AXES, split_axis=0, concat_axis=0, axis_index_group...  34.7 us
    pallas_call x1, Pallas kernels, local(): call(conv_kernel, devices, flat, (wide, wide))(arrived, *constants)  1.34 us
    pallas_call x1, Pallas kernels, local(): arrived = exchange(gate(*operands))  1.33 us
    pallas_call x1, Pallas kernels, local(): return tuple(finish(returned, keys, values, cotangent))  0.92 us

profile of v5, /device:TPU:1, one launch (start us, length us, event | category | flops | bytes accessed | tf_op | source)
XLA Modules:
  0.0 39.1 jit_solution(5828736207588500662)
XLA Ops:
  0.6 1.3 %shard_map.129 = f32[768,128]{1,0:T(8,128)S(1)} custom-call(f32[1,128]{1,0:T(1,128)} %bitcast.9, f32[256,128]{1,0:T(8,128)} %refs_1_.3, f32[256,128]{1,0:T(8,128)} %refs_1_.4, f32[256,128]{1,0:T(8,128)} %refs_2_.4, f32[256,128]{1,0:T(8,128)} %refs_3_.4, f32[256,128]{1,0:T(8,128)} %refs_5_.1), custom_call_target="tpu_custom_call" | custom-call | tf_op jit(solution)/shard_map/pallas_call | solution.py:250
  2.0 0.0 copy-start.3
  2.0 0.0 copy-start.4
  2.0 0.0 copy-start.5
  2.0 0.0 copy-start.6
  2.0 19.6 %all_to_all.22 = f32[32,24,128]{2,1,0:T(8,128)S(1)} all-to-all(f32[32,24,128]{2,1,0:T(8,128)S(1)} %bitcast.8), channel_id=1, replica_groups={{0,24,16,8,1,25,17,9,2,26,18,10,3,27,19,11,4,28,20,12,5,29,21,13,6,30,2..., dimensions={0} | all-to-all | bytes 786432 | tf_op jit(solution)/shard_map/all_to_all | solution.py:237
  21.7 0.0 copy-done.3
  21.7 0.0 copy-done.4
  21.7 0.0 copy-done.5
  21.7 0.0 copy-done.6
  21.7 1.3 %shard_map.130 = f32[768,128]{1,0:T(8,128)S(1)} custom-call(f32[768,128]{1,0:T(8,128)S(1)} %bitcast.6, bf16[128,192]{1,0:T(8,128)(2,1)S(1)} %copy-done.5, f32[2,64,128]{2,1,0:T(8,128)S(1)} %copy-done.4, bf16[2,256,256]{2,1,0:T(8,128)(2,1)S(1)} %copy-done.3, bf16[64,384]{1,0:T(8,128)(2,1)S(1)} %copy-done.6), custom_call_target="tpu_custom_call" | custom-call | tf_op jit(solution)/shard_map/pallas_call | solution.py:253
  23.0 0.0 copy-start
  23.1 0.0 copy-start.1
  23.1 0.0 copy-start.2
  23.1 15.1 %all_to_all.23 = f32[32,24,128]{2,1,0:T(8,128)S(1)} all-to-all(f32[32,24,128]{2,1,0:T(8,128)S(1)} %bitcast.7), channel_id=1, replica_groups={{0,24,16,8,1,25,17,9,2,26,18,10,3,27,19,11,4,28,20,12,5,29,21,13,6,30,2..., dimensions={0} | all-to-all | bytes 786432 | tf_op jit(solution)/shard_map/all_to_all | solution.py:237
  38.2 0.0 copy-done
  38.2 0.0 copy-done.1
  38.2 0.0 copy-done.2
  38.2 0.9 %shard_map.131 = (f32[256,128]{1,0:T(8,128)}, f32[256,128]{1,0:T(8,128)}, f32[256,128]{1,0:T(8,128)}, f32[256,128]{1,0:T(8,128)}) custom-call(f32[768,128]{1,0:T(8,128)S(1)} %bitcast.5, f32[256,128]{1,0:T(8,128)S(1)} %copy-done, f32[256,128]{1,0:T(8,128)S(1)} %copy-done.1, f32[256,128]{1,0:T(8,128)S(1)} %copy-done.2), custom_call_target="tpu_custom_call" | custom-call | tf_op jit(solution)/shard_map/pallas_call | solution.py:263
Async XLA Ops:
  2.0 19.7 %copy-start.3 = (bf16[2,256,256]{2,1,0:T(8,128)(2,1)S(1)}, bf16[2,256,256]{2,1,0:T(8,128)(2,1)}, u32[]{:S(2)}) copy-start(bf16[2,256,256]{2,1,0:T(8,128)(2,1)} %constant.10.clone.refs_3_) | copy-start | bytes 786436
  2.0 19.7 %copy-start.4 = (f32[2,64,128]{2,1,0:T(8,128)S(1)}, f32[2,64,128]{2,1,0:T(8,128)}, u32[]{:S(2)}) copy-start(f32[2,64,128]{2,1,0:T(8,128)} %constant.9.clone.refs_2_) | copy-start | bytes 196612
  2.0 19.7 %copy-start.5 = (bf16[128,192]{1,0:T(8,128)(2,1)S(1)}, bf16[128,192]{1,0:T(8,128)(2,1)}, u32[]{:S(2)}) copy-start(bf16[128,192]{1,0:T(8,128)(2,1)} %constant.8.clone.refs_1_) | copy-start | bytes 147460
  2.0 19.7 %copy-start.6 = (bf16[64,384]{1,0:T(8,128)(2,1)S(1)}, bf16[64,384]{1,0:T(8,128)(2,1)}, u32[]{:S(2)}) copy-start(bf16[64,384]{1,0:T(8,128)(2,1)} %constant.11.clone.refs_4_) | copy-start | bytes 147460
  23.0 15.1 %copy-start = (f32[256,128]{1,0:T(8,128)S(1)}, f32[256,128]{1,0:T(8,128)}, u32[]{:S(2)}) copy-start(f32[256,128]{1,0:T(8,128)} %refs_1_.4) | copy-start | bytes 393220
  23.1 15.1 %copy-start.1 = (f32[256,128]{1,0:T(8,128)S(1)}, f32[256,128]{1,0:T(8,128)}, u32[]{:S(2)}) copy-start(f32[256,128]{1,0:T(8,128)} %refs_2_.4) | copy-start | bytes 393220
  23.1 15.1 %copy-start.2 = (f32[256,128]{1,0:T(8,128)S(1)}, f32[256,128]{1,0:T(8,128)}, u32[]{:S(2)}) copy-start(f32[256,128]{1,0:T(8,128)} %refs_3_.4) | copy-start | bytes 393220

commit v6 on v5

--- a/solution.py
+++ b/solution.py
@@ -21,7 +21,7 @@
 
 
 def exchange_order(planes, width):
-    return [-plane % planes * width + place for place in range(width) for plane in range(planes)]
+    return [(1 - plane) % planes * width + place for place in range(width) for plane in range(planes)]
 
 
 def tables(tokens, devices, group):

time: 39.3 us -> 39.7 us (1.010)
  blocking collectives: 34.7 us -> 35.1 us
where the time goes in v6:
time: 39.7 us; the launch traced here: 39.5 us
  blocking collectives  35.1 us (88%)
  Pallas kernels  3.59 us (9%)
  between operations  0.72 us (2%)
    all_to_all x2, blocking collectives, exchange(): lax.all_to_all(array, AXES, split_axis=0, concat_axis=0, axis_index_group...  35.1 us
    pallas_call x1, Pallas kernels, local(): call(conv_kernel, devices, flat, (wide, wide))(arrived, *constants)  1.34 us
    pallas_call x1, Pallas kernels, local(): arrived = exchange(gate(*operands))  1.33 us
    pallas_call x1, Pallas kernels, local(): return tuple(finish(returned, keys, values, cotangent))  0.92 us

profile of v6, /device:TPU:1, one launch (start us, length us, event | category | flops | bytes accessed | tf_op | source)
XLA Modules:
  0.0 39.5 jit_solution(8639844241817033630)
XLA Ops:
  0.6 1.3 %shard_map.129 = f32[768,128]{1,0:T(8,128)S(1)} custom-call(f32[1,128]{1,0:T(1,128)} %bitcast.9, f32[256,128]{1,0:T(8,128)} %refs_1_.3, f32[256,128]{1,0:T(8,128)} %refs_1_.4, f32[256,128]{1,0:T(8,128)} %refs_2_.4, f32[256,128]{1,0:T(8,128)} %refs_3_.4, f32[256,128]{1,0:T(8,128)} %refs_5_.1), custom_call_target="tpu_custom_call" | custom-call | tf_op jit(solution)/shard_map/pallas_call | solution.py:250
  2.0 0.0 copy-start.3
  2.0 0.0 copy-start.4
  2.0 0.0 copy-start.5
  2.0 0.0 copy-start.6
  2.0 19.6 %all_to_all.22 = f32[32,24,128]{2,1,0:T(8,128)S(1)} all-to-all(f32[32,24,128]{2,1,0:T(8,128)S(1)} %bitcast.8), channel_id=1, replica_groups={{8,0,24,16,9,1,25,17,10,2,26,18,11,3,27,19,12,4,28,20,13,5,29,21,14,6,3..., dimensions={0} | all-to-all | bytes 786432 | tf_op jit(solution)/shard_map/all_to_all | solution.py:237
  21.7 0.0 copy-done.3
  21.7 0.0 copy-done.4
  21.7 0.0 copy-done.5
  21.7 0.0 copy-done.6
  21.7 1.3 %shard_map.130 = f32[768,128]{1,0:T(8,128)S(1)} custom-call(f32[768,128]{1,0:T(8,128)S(1)} %bitcast.6, bf16[128,192]{1,0:T(8,128)(2,1)S(1)} %copy-done.5, f32[2,64,128]{2,1,0:T(8,128)S(1)} %copy-done.4, bf16[2,256,256]{2,1,0:T(8,128)(2,1)S(1)} %copy-done.3, bf16[64,384]{1,0:T(8,128)(2,1)S(1)} %copy-done.6), custom_call_target="tpu_custom_call" | custom-call | tf_op jit(solution)/shard_map/pallas_call | solution.py:253
  23.0 0.0 copy-start
  23.1 0.0 copy-start.1
  23.1 0.0 copy-start.2
  23.1 15.5 %all_to_all.23 = f32[32,24,128]{2,1,0:T(8,128)S(1)} all-to-all(f32[32,24,128]{2,1,0:T(8,128)S(1)} %bitcast.7), channel_id=1, replica_groups={{8,0,24,16,9,1,25,17,10,2,26,18,11,3,27,19,12,4,28,20,13,5,29,21,14,6,3..., dimensions={0} | all-to-all | bytes 786432 | tf_op jit(solution)/shard_map/all_to_all | solution.py:237
  38.6 0.0 copy-done
  38.6 0.0 copy-done.1
  38.6 0.0 copy-done.2
  38.6 0.9 %shard_map.131 = (f32[256,128]{1,0:T(8,128)}, f32[256,128]{1,0:T(8,128)}, f32[256,128]{1,0:T(8,128)}, f32[256,128]{1,0:T(8,128)}) custom-call(f32[768,128]{1,0:T(8,128)S(1)} %bitcast.5, f32[256,128]{1,0:T(8,128)S(1)} %copy-done, f32[256,128]{1,0:T(8,128)S(1)} %copy-done.1, f32[256,128]{1,0:T(8,128)S(1)} %copy-done.2), custom_call_target="tpu_custom_call" | custom-call | tf_op jit(solution)/shard_map/pallas_call | solution.py:263
Async XLA Ops:
  2.0 19.7 %copy-start.3 = (bf16[2,256,256]{2,1,0:T(8,128)(2,1)S(1)}, bf16[2,256,256]{2,1,0:T(8,128)(2,1)}, u32[]{:S(2)}) copy-start(bf16[2,256,256]{2,1,0:T(8,128)(2,1)} %constant.10.clone.refs_3_) | copy-start | bytes 786436
  2.0 19.7 %copy-start.4 = (f32[2,64,128]{2,1,0:T(8,128)S(1)}, f32[2,64,128]{2,1,0:T(8,128)}, u32[]{:S(2)}) copy-start(f32[2,64,128]{2,1,0:T(8,128)} %constant.9.clone.refs_2_) | copy-start | bytes 196612
  2.0 19.7 %copy-start.5 = (bf16[128,192]{1,0:T(8,128)(2,1)S(1)}, bf16[128,192]{1,0:T(8,128)(2,1)}, u32[]{:S(2)}) copy-start(bf16[128,192]{1,0:T(8,128)(2,1)} %constant.8.clone.refs_1_) | copy-start | bytes 147460
  2.0 19.7 %copy-start.6 = (bf16[64,384]{1,0:T(8,128)(2,1)S(1)}, bf16[64,384]{1,0:T(8,128)(2,1)}, u32[]{:S(2)}) copy-start(bf16[64,384]{1,0:T(8,128)(2,1)} %constant.11.clone.refs_4_) | copy-start | bytes 147460
  23.0 15.5 %copy-start = (f32[256,128]{1,0:T(8,128)S(1)}, f32[256,128]{1,0:T(8,128)}, u32[]{:S(2)}) copy-start(f32[256,128]{1,0:T(8,128)} %refs_1_.4) | copy-start | bytes 393220
  23.1 15.5 %copy-start.1 = (f32[256,128]{1,0:T(8,128)S(1)}, f32[256,128]{1,0:T(8,128)}, u32[]{:S(2)}) copy-start(f32[256,128]{1,0:T(8,128)} %refs_2_.4) | copy-start | bytes 393220
  23.1 15.5 %copy-start.2 = (f32[256,128]{1,0:T(8,128)S(1)}, f32[256,128]{1,0:T(8,128)}, u32[]{:S(2)}) copy-start(f32[256,128]{1,0:T(8,128)} %refs_3_.4) | copy-start | bytes 393220

commit v7 on v6

--- a/solution.py
+++ b/solution.py
@@ -21,7 +21,10 @@
 
 
 def exchange_order(planes, width):
-    return [(1 - plane) % planes * width + place for place in range(width) for plane in range(planes)]
+    chips = width // 2
+    walk = [chip for start in range(2) for chip in range(start, chips, 2)]
+    places = [chip * 2 + core for chip in walk for core in range(2)]
+    return [-plane % planes * width + place for place in places for plane in range(planes)]
 
 
 def tables(tokens, devices, group):

time: 39.7 us -> 39.3 us (0.990)
  blocking collectives: 35.1 us -> 34.7 us
where the time goes in v7:
time: 39.3 us; the launch traced here: 39.1 us
  blocking collectives  34.7 us (88%)
  Pallas kernels  3.59 us (9%)
  between operations  0.72 us (2%)
    all_to_all x2, blocking collectives, exchange(): lax.all_to_all(array, AXES, split_axis=0, concat_axis=0, axis_index_group...  34.7 us
    pallas_call x1, Pallas kernels, local(): call(conv_kernel, devices, flat, (wide, wide))(arrived, *constants)  1.34 us
    pallas_call x1, Pallas kernels, local(): arrived = exchange(gate(*operands))  1.33 us
    pallas_call x1, Pallas kernels, local(): return tuple(finish(returned, keys, values, cotangent))  0.92 us

profile of v7, /device:TPU:1, one launch (start us, length us, event | category | flops | bytes accessed | tf_op | source)
XLA Modules:
  0.0 39.1 jit_solution(6284796180082982166)
XLA Ops:
  0.6 1.3 %shard_map.129 = f32[768,128]{1,0:T(8,128)S(1)} custom-call(f32[1,128]{1,0:T(1,128)} %bitcast.9, f32[256,128]{1,0:T(8,128)} %refs_1_.3, f32[256,128]{1,0:T(8,128)} %refs_1_.4, f32[256,128]{1,0:T(8,128)} %refs_2_.4, f32[256,128]{1,0:T(8,128)} %refs_3_.4, f32[256,128]{1,0:T(8,128)} %refs_5_.1), custom_call_target="tpu_custom_call" | custom-call | tf_op jit(solution)/shard_map/pallas_call | solution.py:253
  2.0 0.0 copy-start.3
  2.0 0.0 copy-start.4
  2.0 0.0 copy-start.5
  2.0 0.0 copy-start.6
  2.0 19.6 %all_to_all.22 = f32[32,24,128]{2,1,0:T(8,128)S(1)} all-to-all(f32[32,24,128]{2,1,0:T(8,128)S(1)} %bitcast.8), channel_id=1, replica_groups={{0,24,16,8,1,25,17,9,4,28,20,12,5,29,21,13,2,26,18,10,3,27,19,11,6,30,2..., dimensions={0} | all-to-all | bytes 786432 | tf_op jit(solution)/shard_map/all_to_all | solution.py:240
  21.7 0.0 copy-done.3
  21.7 0.0 copy-done.4
  21.7 0.0 copy-done.5
  21.7 0.0 copy-done.6
  21.7 1.3 %shard_map.130 = f32[768,128]{1,0:T(8,128)S(1)} custom-call(f32[768,128]{1,0:T(8,128)S(1)} %bitcast.6, bf16[128,192]{1,0:T(8,128)(2,1)S(1)} %copy-done.5, f32[2,64,128]{2,1,0:T(8,128)S(1)} %copy-done.4, bf16[2,256,256]{2,1,0:T(8,128)(2,1)S(1)} %copy-done.3, bf16[64,384]{1,0:T(8,128)(2,1)S(1)} %copy-done.6), custom_call_target="tpu_custom_call" | custom-call | tf_op jit(solution)/shard_map/pallas_call | solution.py:256
  23.0 0.0 copy-start
  23.1 0.0 copy-start.1
  23.1 0.0 copy-start.2
  23.1 15.1 %all_to_all.23 = f32[32,24,128]{2,1,0:T(8,128)S(1)} all-to-all(f32[32,24,128]{2,1,0:T(8,128)S(1)} %bitcast.7), channel_id=1, replica_groups={{0,24,16,8,1,25,17,9,4,28,20,12,5,29,21,13,2,26,18,10,3,27,19,11,6,30,2..., dimensions={0} | all-to-all | bytes 786432 | tf_op jit(solution)/shard_map/all_to_all | solution.py:240
  38.2 0.0 copy-done
  38.2 0.0 copy-done.1
  38.2 0.0 copy-done.2
  38.2 0.9 %shard_map.131 = (f32[256,128]{1,0:T(8,128)}, f32[256,128]{1,0:T(8,128)}, f32[256,128]{1,0:T(8,128)}, f32[256,128]{1,0:T(8,128)}) custom-call(f32[768,128]{1,0:T(8,128)S(1)} %bitcast.5, f32[256,128]{1,0:T(8,128)S(1)} %copy-done, f32[256,128]{1,0:T(8,128)S(1)} %copy-done.1, f32[256,128]{1,0:T(8,128)S(1)} %copy-done.2), custom_call_target="tpu_custom_call" | custom-call | tf_op jit(solution)/shard_map/pallas_call | solution.py:266
Async XLA Ops:
  2.0 19.7 %copy-start.3 = (bf16[2,256,256]{2,1,0:T(8,128)(2,1)S(1)}, bf16[2,256,256]{2,1,0:T(8,128)(2,1)}, u32[]{:S(2)}) copy-start(bf16[2,256,256]{2,1,0:T(8,128)(2,1)} %constant.10.clone.refs_3_) | copy-start | bytes 786436
  2.0 19.7 %copy-start.4 = (f32[2,64,128]{2,1,0:T(8,128)S(1)}, f32[2,64,128]{2,1,0:T(8,128)}, u32[]{:S(2)}) copy-start(f32[2,64,128]{2,1,0:T(8,128)} %constant.9.clone.refs_2_) | copy-start | bytes 196612
  2.0 19.7 %copy-start.5 = (bf16[128,192]{1,0:T(8,128)(2,1)S(1)}, bf16[128,192]{1,0:T(8,128)(2,1)}, u32[]{:S(2)}) copy-start(bf16[128,192]{1,0:T(8,128)(2,1)} %constant.8.clone.refs_1_) | copy-start | bytes 147460
  2.0 19.7 %copy-start.6 = (bf16[64,384]{1,0:T(8,128)(2,1)S(1)}, bf16[64,384]{1,0:T(8,128)(2,1)}, u32[]{:S(2)}) copy-start(bf16[64,384]{1,0:T(8,128)(2,1)} %constant.11.clone.refs_4_) | copy-start | bytes 147460
  23.0 15.1 %copy-start = (f32[256,128]{1,0:T(8,128)S(1)}, f32[256,128]{1,0:T(8,128)}, u32[]{:S(2)}) copy-start(f32[256,128]{1,0:T(8,128)} %refs_1_.4) | copy-start | bytes 393220
  23.1 15.1 %copy-start.1 = (f32[256,128]{1,0:T(8,128)S(1)}, f32[256,128]{1,0:T(8,128)}, u32[]{:S(2)}) copy-start(f32[256,128]{1,0:T(8,128)} %refs_2_.4) | copy-start | bytes 393220
  23.1 15.1 %copy-start.2 = (f32[256,128]{1,0:T(8,128)S(1)}, f32[256,128]{1,0:T(8,128)}, u32[]{:S(2)}) copy-start(f32[256,128]{1,0:T(8,128)} %refs_3_.4) | copy-start | bytes 393220

commit v8 on v6

--- a/solution.py
+++ b/solution.py
@@ -21,7 +21,12 @@
 
 
 def exchange_order(planes, width):
-    return [(1 - plane) % planes * width + place for place in range(width) for plane in range(planes)]
+    return [
+        -plane % planes * width + chip * 2 + core
+        for chip in range(width // 2)
+        for plane in range(planes)
+        for core in range(2)
+    ]
 
 
 def tables(tokens, devices, group):

time: 39.7 us -> 40.6 us (1.023)
  the two profiles are of different devices: /device:TPU:1 before, /device:TPU:0 now
where the time goes in v8:
time: 40.6 us; the launch traced here: 40.4 us
  blocking collectives  36 us (89%)
  Pallas kernels  3.6 us (9%)
  between operations  0.72 us (2%)
    all_to_all x2, blocking collectives, exchange(): lax.all_to_all(array, AXES, split_axis=0, concat_axis=0, axis_index_group...  36 us
    pallas_call x1, Pallas kernels, local(): call(conv_kernel, devices, flat, (wide, wide))(arrived, *constants)  1.34 us
    pallas_call x1, Pallas kernels, local(): arrived = exchange(gate(*operands))  1.33 us
    pallas_call x1, Pallas kernels, local(): return tuple(finish(returned, keys, values, cotangent))  0.92 us

profile of v8, /device:TPU:0, one launch (start us, length us, event | category | flops | bytes accessed | tf_op | source)
XLA Modules:
  0.0 40.4 jit_solution(10688136611870128951)
XLA Ops:
  0.6 1.3 %shard_map.129 = f32[768,128]{1,0:T(8,128)S(1)} custom-call(f32[1,128]{1,0:T(1,128)} %bitcast.9, f32[256,128]{1,0:T(8,128)} %refs_1_.3, f32[256,128]{1,0:T(8,128)} %refs_1_.4, f32[256,128]{1,0:T(8,128)} %refs_2_.4, f32[256,128]{1,0:T(8,128)} %refs_3_.4, f32[256,128]{1,0:T(8,128)} %refs_5_.1), custom_call_target="tpu_custom_call" | custom-call | tf_op jit(solution)/shard_map/pallas_call | solution.py:255
  2.0 0.0 copy-start.3
  2.0 0.0 copy-start.4
  2.0 0.0 copy-start.5
  2.0 0.0 copy-start.6
  2.0 20.6 %all_to_all.22 = f32[32,24,128]{2,1,0:T(8,128)S(1)} all-to-all(f32[32,24,128]{2,1,0:T(8,128)S(1)} %bitcast.8), channel_id=1, replica_groups={{0,1,24,25,16,17,8,9,2,3,26,27,18,19,10,11,4,5,28,29,20,21,12,13,6,7,30..., dimensions={0} | all-to-all | bytes 786432 | tf_op jit(solution)/shard_map/all_to_all | solution.py:242
  22.7 0.0 copy-done.3
  22.7 0.0 copy-done.4
  22.7 0.0 copy-done.5
  22.7 0.0 copy-done.6
  22.7 1.3 %shard_map.130 = f32[768,128]{1,0:T(8,128)S(1)} custom-call(f32[768,128]{1,0:T(8,128)S(1)} %bitcast.6, bf16[128,192]{1,0:T(8,128)(2,1)S(1)} %copy-done.5, f32[2,64,128]{2,1,0:T(8,128)S(1)} %copy-done.4, bf16[2,256,256]{2,1,0:T(8,128)(2,1)S(1)} %copy-done.3, bf16[64,384]{1,0:T(8,128)(2,1)S(1)} %copy-done.6), custom_call_target="tpu_custom_call" | custom-call | tf_op jit(solution)/shard_map/pallas_call | solution.py:258
  24.0 0.0 copy-start
  24.1 0.0 copy-start.1
  24.1 0.0 copy-start.2
  24.1 15.4 %all_to_all.23 = f32[32,24,128]{2,1,0:T(8,128)S(1)} all-to-all(f32[32,24,128]{2,1,0:T(8,128)S(1)} %bitcast.7), channel_id=1, replica_groups={{0,1,24,25,16,17,8,9,2,3,26,27,18,19,10,11,4,5,28,29,20,21,12,13,6,7,30..., dimensions={0} | all-to-all | bytes 786432 | tf_op jit(solution)/shard_map/all_to_all | solution.py:242
  39.5 0.0 copy-done
  39.5 0.0 copy-done.1
  39.5 0.0 copy-done.2
  39.5 0.9 %shard_map.131 = (f32[256,128]{1,0:T(8,128)}, f32[256,128]{1,0:T(8,128)}, f32[256,128]{1,0:T(8,128)}, f32[256,128]{1,0:T(8,128)}) custom-call(f32[768,128]{1,0:T(8,128)S(1)} %bitcast.5, f32[256,128]{1,0:T(8,128)S(1)} %copy-done, f32[256,128]{1,0:T(8,128)S(1)} %copy-done.1, f32[256,128]{1,0:T(8,128)S(1)} %copy-done.2), custom_call_target="tpu_custom_call" | custom-call | tf_op jit(solution)/shard_map/pallas_call | solution.py:268
Async XLA Ops:
  2.0 20.7 %copy-start.3 = (bf16[2,256,256]{2,1,0:T(8,128)(2,1)S(1)}, bf16[2,256,256]{2,1,0:T(8,128)(2,1)}, u32[]{:S(2)}) copy-start(bf16[2,256,256]{2,1,0:T(8,128)(2,1)} %constant.10.clone.refs_3_) | copy-start | bytes 786436
  2.0 20.7 %copy-start.4 = (f32[2,64,128]{2,1,0:T(8,128)S(1)}, f32[2,64,128]{2,1,0:T(8,128)}, u32[]{:S(2)}) copy-start(f32[2,64,128]{2,1,0:T(8,128)} %constant.9.clone.refs_2_) | copy-start | bytes 196612
  2.0 20.7 %copy-start.5 = (bf16[128,192]{1,0:T(8,128)(2,1)S(1)}, bf16[128,192]{1,0:T(8,128)(2,1)}, u32[]{:S(2)}) copy-start(bf16[128,192]{1,0:T(8,128)(2,1)} %constant.8.clone.refs_1_) | copy-start | bytes 147460
  2.0 20.7 %copy-start.6 = (bf16[64,384]{1,0:T(8,128)(2,1)S(1)}, bf16[64,384]{1,0:T(8,128)(2,1)}, u32[]{:S(2)}) copy-start(bf16[64,384]{1,0:T(8,128)(2,1)} %constant.11.clone.refs_4_) | copy-start | bytes 147460
  24.0 15.4 %copy-start = (f32[256,128]{1,0:T(8,128)S(1)}, f32[256,128]{1,0:T(8,128)}, u32[]{:S(2)}) copy-start(f32[256,128]{1,0:T(8,128)} %refs_1_.4) | copy-start | bytes 393220
  24.1 15.4 %copy-start.1 = (f32[256,128]{1,0:T(8,128)S(1)}, f32[256,128]{1,0:T(8,128)}, u32[]{:S(2)}) copy-start(f32[256,128]{1,0:T(8,128)} %refs_2_.4) | copy-start | bytes 393220
  24.1 15.4 %copy-start.2 = (f32[256,128]{1,0:T(8,128)S(1)}, f32[256,128]{1,0:T(8,128)}, u32[]{:S(2)}) copy-start(f32[256,128]{1,0:T(8,128)} %refs_3_.4) | copy-start | bytes 393220

commit v9 on v7

--- a/solution.py
+++ b/solution.py
@@ -22,7 +22,7 @@
 
 def exchange_order(planes, width):
     chips = width // 2
-    walk = [chip for start in range(2) for chip in range(start, chips, 2)]
+    walk = [chip ^ (chip >> 1) ^ (chips // 2) for chip in range(chips)]
     places = [chip * 2 + core for chip in walk for core in range(2)]
     return [-plane % planes * width + place for place in places for plane in range(planes)]
 

time: 39.3 us -> 39.7 us (1.010)
  blocking collectives: 34.7 us -> 35.2 us
    all_to_all x2, blocking collectives: 34.7 us -> 35.2 us  [exchange(): lax.all_to_all(array, AXES, split_axis=0, concat_axis=0, axis_index_group...]
where the time goes in v9:
time: 39.7 us; the launch traced here: 39.6 us
  blocking collectives  35.2 us (89%)
  Pallas kernels  3.6 us (9%)
  between operations  0.72 us (2%)
    all_to_all x2, blocking collectives, exchange(): lax.all_to_all(array, AXES, split_axis=0, concat_axis=0, axis_index_group...  35.2 us
    pallas_call x1, Pallas kernels, local(): call(conv_kernel, devices, flat, (wide, wide))(arrived, *constants)  1.34 us
    pallas_call x1, Pallas kernels, local(): arrived = exchange(gate(*operands))  1.33 us
    pallas_call x1, Pallas kernels, local(): return tuple(finish(returned, keys, values, cotangent))  0.92 us

profile of v9, /device:TPU:1, one launch (start us, length us, event | category | flops | bytes accessed | tf_op | source)
XLA Modules:
  0.0 39.6 jit_solution(17001518419797128360)
XLA Ops:
  0.6 1.3 %shard_map.129 = f32[768,128]{1,0:T(8,128)S(1)} custom-call(f32[1,128]{1,0:T(1,128)} %bitcast.9, f32[256,128]{1,0:T(8,128)} %refs_1_.3, f32[256,128]{1,0:T(8,128)} %refs_1_.4, f32[256,128]{1,0:T(8,128)} %refs_2_.4, f32[256,128]{1,0:T(8,128)} %refs_3_.4, f32[256,128]{1,0:T(8,128)} %refs_5_.1), custom_call_target="tpu_custom_call" | custom-call | tf_op jit(solution)/shard_map/pallas_call | solution.py:253
  2.0 0.0 copy-start.3
  2.0 0.0 copy-start.4
  2.0 0.0 copy-start.5
  2.0 0.0 copy-start.6
  2.0 20.1 %all_to_all.22 = f32[32,24,128]{2,1,0:T(8,128)S(1)} all-to-all(f32[32,24,128]{2,1,0:T(8,128)S(1)} %bitcast.8), channel_id=1, replica_groups={{4,28,20,12,5,29,21,13,6,30,22,14,7,31,23,15,2,26,18,10,3,27,19,11,0,24..., dimensions={0} | all-to-all | bytes 786432 | tf_op jit(solution)/shard_map/all_to_all | solution.py:240
  22.1 0.0 copy-done.3
  22.1 0.0 copy-done.4
  22.1 0.0 copy-done.5
  22.1 0.0 copy-done.6
  22.1 1.3 %shard_map.130 = f32[768,128]{1,0:T(8,128)S(1)} custom-call(f32[768,128]{1,0:T(8,128)S(1)} %bitcast.6, bf16[128,192]{1,0:T(8,128)(2,1)S(1)} %copy-done.5, f32[2,64,128]{2,1,0:T(8,128)S(1)} %copy-done.4, bf16[2,256,256]{2,1,0:T(8,128)(2,1)S(1)} %copy-done.3, bf16[64,384]{1,0:T(8,128)(2,1)S(1)} %copy-done.6), custom_call_target="tpu_custom_call" | custom-call | tf_op jit(solution)/shard_map/pallas_call | solution.py:256
  23.5 0.0 copy-start
  23.5 0.0 copy-start.1
  23.5 0.0 copy-start.2
  23.5 15.1 %all_to_all.23 = f32[32,24,128]{2,1,0:T(8,128)S(1)} all-to-all(f32[32,24,128]{2,1,0:T(8,128)S(1)} %bitcast.7), channel_id=1, replica_groups={{4,28,20,12,5,29,21,13,6,30,22,14,7,31,23,15,2,26,18,10,3,27,19,11,0,24..., dimensions={0} | all-to-all | bytes 786432 | tf_op jit(solution)/shard_map/all_to_all | solution.py:240
  38.6 0.0 copy-done
  38.6 0.0 copy-done.1
  38.6 0.0 copy-done.2
  38.6 0.9 %shard_map.131 = (f32[256,128]{1,0:T(8,128)}, f32[256,128]{1,0:T(8,128)}, f32[256,128]{1,0:T(8,128)}, f32[256,128]{1,0:T(8,128)}) custom-call(f32[768,128]{1,0:T(8,128)S(1)} %bitcast.5, f32[256,128]{1,0:T(8,128)S(1)} %copy-done, f32[256,128]{1,0:T(8,128)S(1)} %copy-done.1, f32[256,128]{1,0:T(8,128)S(1)} %copy-done.2), custom_call_target="tpu_custom_call" | custom-call | tf_op jit(solution)/shard_map/pallas_call | solution.py:266
Async XLA Ops:
  2.0 20.2 %copy-start.3 = (bf16[2,256,256]{2,1,0:T(8,128)(2,1)S(1)}, bf16[2,256,256]{2,1,0:T(8,128)(2,1)}, u32[]{:S(2)}) copy-start(bf16[2,256,256]{2,1,0:T(8,128)(2,1)} %constant.10.clone.refs_3_) | copy-start | bytes 786436
  2.0 20.1 %copy-start.4 = (f32[2,64,128]{2,1,0:T(8,128)S(1)}, f32[2,64,128]{2,1,0:T(8,128)}, u32[]{:S(2)}) copy-start(f32[2,64,128]{2,1,0:T(8,128)} %constant.9.clone.refs_2_) | copy-start | bytes 196612
  2.0 20.1 %copy-start.5 = (bf16[128,192]{1,0:T(8,128)(2,1)S(1)}, bf16[128,192]{1,0:T(8,128)(2,1)}, u32[]{:S(2)}) copy-start(bf16[128,192]{1,0:T(8,128)(2,1)} %constant.8.clone.refs_1_) | copy-start | bytes 147460
  2.0 20.1 %copy-start.6 = (bf16[64,384]{1,0:T(8,128)(2,1)S(1)}, bf16[64,384]{1,0:T(8,128)(2,1)}, u32[]{:S(2)}) copy-start(bf16[64,384]{1,0:T(8,128)(2,1)} %constant.11.clone.refs_4_) | copy-start | bytes 147460
  23.5 15.1 %copy-start = (f32[256,128]{1,0:T(8,128)S(1)}, f32[256,128]{1,0:T(8,128)}, u32[]{:S(2)}) copy-start(f32[256,128]{1,0:T(8,128)} %refs_1_.4) | copy-start | bytes 393220
  23.5 15.1 %copy-start.1 = (f32[256,128]{1,0:T(8,128)S(1)}, f32[256,128]{1,0:T(8,128)}, u32[]{:S(2)}) copy-start(f32[256,128]{1,0:T(8,128)} %refs_2_.4) | copy-start | bytes 393220
  23.5 15.1 %copy-start.2 = (f32[256,128]{1,0:T(8,128)S(1)}, f32[256,128]{1,0:T(8,128)}, u32[]{:S(2)}) copy-start(f32[256,128]{1,0:T(8,128)} %refs_3_.4) | copy-start | bytes 393220
